TPU v7x, 32 devices: a whole 2x2x4 slice. The times are simulated.
32 devices in a mesh: smp: 4 (over x, core), ctx: 8 (over z, y).
Axes of the slice: x: 2, y: 2, z: 4, core: 2. Of those that a mesh axis runs over, the one named last changes fastest.
Arguments:
- query: bfloat16 [4, 1024, 4096], P('smp', 'ctx'), may hold values from -6 to 6
- d_out: bfloat16 [4, 1024, 4096], P('smp', 'ctx'), may hold values from -6 to 6
- branch_kv: bfloat16 [4, 1024, 1024], P('smp', 'ctx'), may hold values from -6 to 6
- prefix_kv: bfloat16 [256, 1024], P('ctx', 'smp'), may hold values from -6 to 6
- parents: int32 [4, 8], P('smp'), may hold values from -1 to 6, as said below
- lengths: int32 [4, 8], P('smp'), may hold values from 33 to 128, as said below
Outputs:
- attn_out: bfloat16 [4, 1024, 4096], P('smp', 'ctx')
- d_query: bfloat16 [4, 1024, 4096], P('smp', 'ctx')
- d_branch_kv: bfloat16 [4, 1024, 1024], P('smp', 'ctx')
- d_prefix_kv: bfloat16 [256, 1024], P('ctx', 'smp')
Inputs may be any that keep to these rules, and one draw needn't show every extreme that they name: parents[s, 0] = -1; for i > 0 parents[s, i] lies below i; every path from the prefix to a block has at most 4 blocks, the block included, and block 3 of every sample has exactly 4; parents[s, 7] = 6. lengths[s, 0] = 128 and lengths[s, 1] = 33.
All inputs are finite; a program needn't handle non-finite values.
Results may differ from a plain program's by a relative error of at most 0.03.
Values may be sent and summed in bfloat16 or wider, within the bound.
A program may use at most 128 MiB of HBM per device.

v0:
```python
import jax
import jax.numpy as jnp
from jax import lax
from jax.sharding import PartitionSpec as P

HK = 4
HD = 128


def build_masks(parent_row, length_row, block_index, depth_slots, block_rows, prefix_rows):
    num_blocks = parent_row.shape[0]
    indices = jnp.arange(num_blocks, dtype=jnp.int32)
    parent_links = (parent_row[:, None] == indices[None, :]).astype(jnp.float32)
    reachable = jnp.eye(num_blocks, dtype=jnp.float32) + parent_links
    for _ in range(num_blocks.bit_length()):
        reachable = jnp.minimum(jnp.dot(reachable, reachable, precision=lax.Precision.HIGHEST), 1.0)
    pick_row = (indices == block_index).astype(jnp.float32)
    ancestry = jnp.dot(pick_row, reachable, precision=lax.Precision.HIGHEST)
    position = jnp.cumsum(ancestry) - 1.0
    slot_ids = jnp.arange(depth_slots, dtype=jnp.float32)
    selector = ancestry[None, :] * (position[None, :] == slot_ids[:, None]).astype(jnp.float32)
    block_float = indices.astype(jnp.float32)
    owner_block = jnp.dot(selector, block_float, precision=lax.Precision.HIGHEST)
    slot_used = jnp.sum(selector, axis=1) > 0.5
    own_slot = slot_used & (jnp.abs(owner_block - jnp.sum(pick_row * block_float)) < 0.5)
    lengths_float = length_row.astype(jnp.float32)
    slot_length = jnp.dot(selector, lengths_float, precision=lax.Precision.HIGHEST)
    own_length = jnp.sum(pick_row * lengths_float)
    place = jnp.arange(block_rows, dtype=jnp.float32)
    row_place = place[:, None, None]
    key_place = place[None, None, :]
    slot_allowed = (
        slot_used[None, :, None]
        & (key_place < slot_length[None, :, None])
        & (jnp.logical_not(own_slot)[None, :, None] | (key_place <= row_place))
    )
    key_allowed = jnp.concatenate(
        [
            jnp.ones((block_rows, prefix_rows), dtype=jnp.bool_),
            slot_allowed.reshape(block_rows, depth_slots * block_rows),
        ],
        axis=1,
    )
    row_valid = place < own_length
    return (selector, key_allowed, row_valid)


def attend(query_block, dout_block, key_values, key_allowed, row_valid, heads_kv, head_dim):
    row_count = query_block.shape[0]
    query_width = query_block.shape[1]
    group_size = query_width // (heads_kv * head_dim)
    key_count = key_values.shape[0]
    softmax_scale = head_dim ** (-0.5)
    grad_live = jnp.where(row_valid[:, None], dout_block, jnp.zeros_like(dout_block))
    query_heads = (
        query_block.reshape(row_count, heads_kv, group_size, head_dim)
        .transpose(1, 0, 2, 3)
        .reshape(heads_kv, row_count * group_size, head_dim)
    )
    grad_heads = (
        grad_live.reshape(row_count, heads_kv, group_size, head_dim)
        .transpose(1, 0, 2, 3)
        .reshape(heads_kv, row_count * group_size, head_dim)
    )
    key_heads = (
        key_values[:, : heads_kv * head_dim]
        .reshape(key_count, heads_kv, head_dim)
        .transpose(1, 0, 2)
    )
    value_heads = (
        key_values[:, heads_kv * head_dim :]
        .reshape(key_count, heads_kv, head_dim)
        .transpose(1, 0, 2)
    )
    mask_rows = jnp.repeat(key_allowed, group_size, axis=0)
    live_rows = jnp.repeat(row_valid, group_size)

    def one_head(inputs):
        query_head, grad_head, key_head, value_head = inputs
        scores = jnp.dot(query_head, key_head.T, preferred_element_type=jnp.float32) * softmax_scale
        scores = jnp.where(mask_rows, scores, -jnp.inf)
        row_max = jnp.max(scores, axis=1, keepdims=True)
        exponent = jnp.exp(scores - row_max)
        probability = exponent / jnp.sum(exponent, axis=1, keepdims=True)
        prob_round = probability.astype(jnp.bfloat16)
        attended = jnp.dot(prob_round, value_head, preferred_element_type=jnp.float32)
        attended_out = jnp.where(live_rows[:, None], attended, 0.0).astype(jnp.bfloat16)
        grad_probs = jnp.dot(grad_head, value_head.T, preferred_element_type=jnp.float32)
        row_delta = jnp.sum(
            grad_head.astype(jnp.float32) * attended_out.astype(jnp.float32), axis=1, keepdims=True
        )
        grad_scores = (probability * (grad_probs - row_delta)).astype(jnp.bfloat16)
        grad_query = (
            jnp.dot(grad_scores, key_head, preferred_element_type=jnp.float32) * softmax_scale
        ).astype(jnp.bfloat16)
        grad_keys = (
            jnp.dot(grad_scores.T, query_head, preferred_element_type=jnp.float32) * softmax_scale
        )
        grad_values = jnp.dot(prob_round.T, grad_head, preferred_element_type=jnp.float32)
        return (attended_out, grad_query, grad_keys, grad_values)

    attended_all, grad_query_all, grad_keys_all, grad_values_all = lax.map(
        one_head, (query_heads, grad_heads, key_heads, value_heads)
    )
    output = (
        attended_all.reshape(heads_kv, row_count, group_size, head_dim)
        .transpose(1, 0, 2, 3)
        .reshape(row_count, query_width)
    )
    grad_query_out = (
        grad_query_all.reshape(heads_kv, row_count, group_size, head_dim)
        .transpose(1, 0, 2, 3)
        .reshape(row_count, query_width)
    )
    grad_pairs = jnp.concatenate(
        [
            grad_keys_all.transpose(1, 0, 2).reshape(key_count, heads_kv * head_dim),
            grad_values_all.transpose(1, 0, 2).reshape(key_count, heads_kv * head_dim),
        ],
        axis=1,
    )
    return (output, grad_query_out, grad_pairs)


def per_device(query, d_out, branch_kv, prefix_kv, parents, lengths):
    num_blocks = parents.shape[1]
    depth_slots = max(4, num_blocks // 4)
    block_rows = query.shape[1]
    block_index = lax.axis_index("ctx")
    with_features = lax.all_gather(prefix_kv, "smp", axis=1, tiled=True)
    prefix_all = lax.all_gather(with_features, "ctx", axis=0, tiled=True)
    prefix_rows = prefix_all.shape[0]
    feature_count = prefix_all.shape[1]
    selector, key_allowed, row_valid = build_masks(
        parents[0], lengths[0], block_index, depth_slots, block_rows, prefix_rows
    )
    selector_low = selector.astype(jnp.bfloat16)
    own_blocks = branch_kv[0]
    all_blocks = lax.all_gather(own_blocks, "ctx", axis=0, tiled=True)
    picked = jnp.einsum(
        "kn,nbf->kbf",
        selector_low,
        all_blocks.reshape(num_blocks, block_rows, feature_count),
        preferred_element_type=jnp.float32,
    ).astype(jnp.bfloat16)
    key_values = jnp.concatenate(
        [prefix_all, picked.reshape(depth_slots * block_rows, feature_count)], axis=0
    )
    output, grad_query, grad_pairs = attend(
        query[0], d_out[0], key_values, key_allowed, row_valid, HK, HD
    )
    grad_prefix = grad_pairs[:prefix_rows]
    slot_grads = grad_pairs[prefix_rows:].reshape(depth_slots, block_rows, feature_count)
    spread = jnp.einsum("km,kbf->mbf", selector, slot_grads, precision=lax.Precision.HIGHEST)
    grad_branch = lax.psum_scatter(
        spread.reshape(block_rows * lax.axis_size("ctx"), feature_count),
        "ctx",
        scatter_dimension=0,
        tiled=True,
    )
    grad_rows = lax.psum_scatter(grad_prefix, "ctx", scatter_dimension=0, tiled=True)
    grad_prefix_out = lax.psum_scatter(grad_rows, "smp", scatter_dimension=1, tiled=True)
    return (
        output[None],
        grad_query[None],
        grad_branch.astype(jnp.bfloat16)[None],
        grad_prefix_out.astype(jnp.bfloat16),
    )


def solution(mesh):
    return jax.shard_map(
        per_device,
        mesh=mesh,
        in_specs=(
            P("smp", "ctx", None),
            P("smp", "ctx", None),
            P("smp", "ctx", None),
            P("ctx", "smp"),
            P("smp", None),
            P("smp", None),
        ),
        out_specs=(
            P("smp", "ctx", None),
            P("smp", "ctx", None),
            P("smp", "ctx", None),
            P("ctx", "smp"),
        ),
        check_vma=False,
    )
```

profile of v0, /device:TPU:0, one launch (start us, length us, event | category | flops | bytes accessed | tf_op | source)
XLA Modules:
  0.0 332.0 jit_solution(15197398757905329553)
XLA Ops:
  15.9 6.2 %all_gather.9 = bf16[32,1024]{1,0:T(8,128)(2,1)S(1)} all-gather(bf16[32,256]{1,0:T(8,128)(2,1)S(1)} %copy-done.8), channel_id=1, replica_groups=mesh['smp'=4,'ctx'=8] {'smp'}, dimensions={1}, use_global_device_ids=true | all-gather | bytes 81920 | tf_op jit(solution)/shard_map/all_gather | solution.py:130
  22.0 33.6 %all_gather.10 = bf16[256,1024]{1,0:T(8,128)(2,1)S(1)} all-gather(bf16[32,1024]{1,0:T(8,128)(2,1)S(1)} %all_gather.9), channel_id=1, replica_groups=mesh['smp'=4,'ctx'=8] {'ctx'}, dimensions={0}, use_global_device_ids=true | all-gather | bytes 589824 | tf_op jit(solution)/shard_map/all_gather | solution.py:131
  55.6 9.9 %all-gather.3.cloned.1.call-done = bf16[1,1024,1024]{2,1,0:T(8,128)(2,1)} async-done(((bf16[1,128,1024]{2,1,0:T(8,128)(2,1)}), bf16[1,1024,1024]{2,1,0:T(8,128)(2,1)}) %all-gather.3.cloned.1.call-update) | async-done | bytes 2097168 | tf_op jit(solution)/shard_map/all_gather | solution.py:139
  65.5 3.0 fusion.37
  71.3 71.6 %while.17 = (s32[]{:T(128)}, bf16[4,1024,128]{2,1,0:T(8,128)(2,1)}, bf16[4,1024,128]{2,1,0:T(8,128)(2,1)}, f32[4,768,128]{2,1,0:T(8,128)}, f32[4,768,128]{2,1,0:...) while((s32[]{:T(128)}, bf16[4,1024,128]{2,1,0:T(8,128)(2,1)}, ...), condition=%wide.region_8.9_spmd.clone, body=%wide.region_4.8_spmd.clone.sunk | while | flops 1219326976 | bytes 45495644 | solution.py:102
  72.7 1.8 fusion.120
  76.8 2.6 multiply_reduce_fusion.2
  81.3 1.9 multiply_convert_fusion.2
  83.2 2.4 fusion.123
  85.6 2.3 fusion.124
  90.6 1.8 fusion.120
  94.7 2.6 multiply_reduce_fusion.2
  99.2 1.9 multiply_convert_fusion.2
  101.0 2.4 fusion.123
  103.5 2.3 fusion.124
  108.6 1.8 fusion.120
  112.6 2.6 multiply_reduce_fusion.2
  117.1 1.9 multiply_convert_fusion.2
  119.0 2.4 fusion.123
  121.4 2.3 fusion.124
  126.5 1.8 fusion.120
  130.5 2.6 multiply_reduce_fusion.2
  135.0 1.9 multiply_convert_fusion.2
  136.9 2.4 fusion.123
  139.3 2.3 fusion.124
  142.9 1.7 bitcast_dynamic-update-slice_fusion.1
  149.5 61.4 %reduce-scatter.6.cloned.1.call-done = f32[32,1024]{1,0:T(8,128)} async-done(((f32[256,1024]{1,0:T(8,128)}), f32[32,1024]{1,0:T(8,128)}) %reduce-scatter.6.cloned.1.call-update) | async-done | bytes 131088 | tf_op jit(solution)/shard_map/reduce_scatter | solution.py:161
  211.1 5.6 %fusion.33 = f32[8,128,1024]{2,0,1:T(8,128)S(1)} fusion(f32[4,128,1024]{2,1,0:T(8,128)S(1)} %bitcast.199, f32[8]{0:T(128)S(1)} %bitcast.216, f32[8]{0:T(128)S(1)} %add_bitcast_fusion), kind=kOutput, calls=%fused_computation.42 | convolution fusion | flops 50331712 | bytes 6291520 | tf_op jit(solution)/shard_map/km,kbf->mbf/dot_general | solution.py:154
  216.7 4.4 %copy.54 = f32[8,128,1024]{2,1,0:T(8,128)} copy(f32[8,128,1024]{2,0,1:T(8,128)S(1)} %fusion.33) | data formatting | bytes 8388608 | tf_op jit(solution)/shard_map/km,kbf->mbf/dot_general | solution.py:154
  225.9 6.1 %reduce-scatter.8.cloned.1.call-done = f32[32,256]{1,0:T(8,128)} async-done(((f32[32,1024]{1,0:T(8,128)}), f32[32,256]{1,0:T(8,128)}) %reduce-scatter.8.cloned.1.call-update) | async-done | bytes 32784 | tf_op jit(solution)/shard_map/reduce_scatter | solution.py:162
  233.4 90.2 %reduce-scatter.4.cloned.1.call-done = f32[128,1024]{1,0:T(8,128)} async-done(((f32[1024,1024]{1,0:T(8,128)}), f32[128,1024]{1,0:T(8,128)}) %reduce-scatter.4.cloned.1.call-update) | async-done | bytes 524304 | tf_op jit(solution)/shard_map/reduce_scatter | solution.py:155
  323.7 1.8 convert_bitcast_fusion
  (133 shorter events, 50.0 us)
Async XLA Ops:
  7.2 58.4 %all-gather.3.cloned.1.call-start = ((), (), s32[]{:S(2)}) async-start(), calls=%async_computation.6 | async-start | bytes 2359296 | tf_op jit(solution)/shard_map/all_gather | solution.py:139
  7.9 203.0 %reduce-scatter.6.cloned.1.call-start = ((), (), s32[]{:S(2)}) async-start(), calls=%async_computation.4 | async-start | bytes 1179648 | tf_op jit(solution)/shard_map/reduce_scatter | solution.py:161
  8.0 2.7 copy-start.5
  9.5 1.8 copy-start.9
  12.6 0.8 copy-start.10
  12.7 3.2 copy-start.8
  71.3 1.4 copy-start.1
  83.1 4.7 %copy-start = (bf16[1024,768]{0,1:T(8,128)(2,1)S(1)}, bf16[1024,768]{0,1:T(8,128)(2,1)}, u32[]{:S(2)}) copy-start(bf16[1024,768]{0,1:T(8,128)(2,1)} %fusion.122) | copy-start | bytes 4718596 | tf_op jit(solution)/shard_map/while
  83.2 4.7 %copy-start.2 = (bf16[4,1024,128]{2,1,0:T(8,128)(2,1)S(1)}, bf16[4,1024,128]{2,1,0:T(8,128)(2,1)}, u32[]{:S(2)}) copy-start(bf16[4,1024,128]{2,1,0:T(8,128)(2,1)} %copy-done.1) | copy-start | bytes 3145732 | tf_op jit(solution)/shard_map/while
  89.2 1.4 copy-start.1
  101.0 4.7 %copy-start = (bf16[1024,768]{0,1:T(8,128)(2,1)S(1)}, bf16[1024,768]{0,1:T(8,128)(2,1)}, u32[]{:S(2)}) copy-start(bf16[1024,768]{0,1:T(8,128)(2,1)} %fusion.122) | copy-start | bytes 4718596 | tf_op jit(solution)/shard_map/while
  101.0 4.7 %copy-start.2 = (bf16[4,1024,128]{2,1,0:T(8,128)(2,1)S(1)}, bf16[4,1024,128]{2,1,0:T(8,128)(2,1)}, u32[]{:S(2)}) copy-start(bf16[4,1024,128]{2,1,0:T(8,128)(2,1)} %copy-done.1) | copy-start | bytes 3145732 | tf_op jit(solution)/shard_map/while
  107.1 1.4 copy-start.1
  119.0 4.7 %copy-start = (bf16[1024,768]{0,1:T(8,128)(2,1)S(1)}, bf16[1024,768]{0,1:T(8,128)(2,1)}, u32[]{:S(2)}) copy-start(bf16[1024,768]{0,1:T(8,128)(2,1)} %fusion.122) | copy-start | bytes 4718596 | tf_op jit(solution)/shard_map/while
  119.0 4.7 %copy-start.2 = (bf16[4,1024,128]{2,1,0:T(8,128)(2,1)S(1)}, bf16[4,1024,128]{2,1,0:T(8,128)(2,1)}, u32[]{:S(2)}) copy-start(bf16[4,1024,128]{2,1,0:T(8,128)(2,1)} %copy-done.1) | copy-start | bytes 3145732 | tf_op jit(solution)/shard_map/while
  125.0 1.4 copy-start.1
  136.9 4.7 %copy-start = (bf16[1024,768]{0,1:T(8,128)(2,1)S(1)}, bf16[1024,768]{0,1:T(8,128)(2,1)}, u32[]{:S(2)}) copy-start(bf16[1024,768]{0,1:T(8,128)(2,1)} %fusion.122) | copy-start | bytes 4718596 | tf_op jit(solution)/shard_map/while
  136.9 4.7 %copy-start.2 = (bf16[4,1024,128]{2,1,0:T(8,128)(2,1)S(1)}, bf16[4,1024,128]{2,1,0:T(8,128)(2,1)}, u32[]{:S(2)}) copy-start(bf16[4,1024,128]{2,1,0:T(8,128)(2,1)} %copy-done.1) | copy-start | bytes 3145732 | tf_op jit(solution)/shard_map/while
  142.9 1.9 copy-start.4
  145.0 1.6 copy-start.3
  147.7 84.3 %reduce-scatter.8.cloned.1.call-start = ((), (), s32[]{:S(2)}) async-start(), calls=%async_computation.5 | async-start | bytes 163840 | tf_op jit(solution)/shard_map/reduce_scatter | solution.py:162
  210.9 112.8 %reduce-scatter.4.cloned.1.call-start = ((), (), s32[]{:S(2)}) async-start(), calls=%async_computation.3 | async-start | bytes 4718592 | tf_op jit(solution)/shard_map/reduce_scatter | solution.py:155
  221.1 1.2 copy-start.6
  222.4 2.1 copy-start.7
Sparse Core Ops, SparseCore 0:
  10.1 55.3 all-gather.2
  147.8 62.9 reduce-scatter.5
  213.4 18.5 reduce-scatter.7
  235.5 88.0 reduce-scatter.3
where the time goes:
time: 333 us; the launch traced here: 332 us
  waiting for transfers between devices  168 us (50%)
  matrix products  59.2 us (18%)
  blocking collectives  39.8 us (12%)
  local copies, waits for them, and re-layouts  36.4 us (11%)
  between operations  14 us (4%)
  other arithmetic  13.6 us (4%)
    reduce_scatter x1, waiting for transfers between devices, per_device(): lax.psum_scatter(spread.reshape(block_rows * lax.axis_size('ctx'), featur...  90.2 us
    reduce_scatter x1, waiting for transfers between devices, per_device(): lax.psum_scatter(grad_prefix, 'ctx', scatter_dimension=0, tiled=True)  61.4 us
    all_gather x1, blocking collectives, per_device(): prefix_all = lax.all_gather(with_features, 'ctx', axis=0, tiled=True)  33.6 us
    dot_general x4, matrix products, one_head(): jnp.dot(prob_round, value_head, preferred_element_type=jnp.float32)  10.5 us
    all_gather x1, waiting for transfers between devices, per_device(): all_blocks = lax.all_gather(own_blocks, 'ctx', axis=0, tiled=True)  9.88 us
    dot_general x4, matrix products, one_head(): jnp.dot(grad_scores, key_head, preferred_element_type=jnp.float32)  9.66 us
    dot_general x4, matrix products, one_head(): jnp.dot(grad_scores.T, query_head, preferred_element_type=jnp.float32)  9.09 us
    unnamed x20, local copies, waits for them, and re-layouts  8.23 us
  transfers between devices with their start and end apart: 4, of which 4 were waited for; matrix products, arithmetic and copies ran while one was open for 7% of the time, Pallas kernels for 0%

commit v1 on v0

v1 whole, which is shorter than its diff:
```python
import functools
import math

import jax
import jax.numpy as jnp
from jax import lax
from jax.experimental import pallas as pl
from jax.experimental.pallas import tpu as pltpu
from jax.sharding import PartitionSpec as P

HK = 4
HD = 128
F32 = jnp.float32
BF16 = jnp.bfloat16


def walk_up(parents, lengths, start, count):
    found = []
    at = start
    for _ in range(count):
        up = parents[0, jnp.maximum(at, 0)]
        at = jnp.where(at >= 0, up, -1)
        held = jnp.maximum(at, 0)
        found.append((held, jnp.where(at >= 0, lengths[0, held], 0), at >= 0))
    return found


def attend_group(query, d_out, keys, values, prefix_rows, own_length, slot_lengths):
    block = query.shape[0]
    group = query.shape[1] // HD
    scale = HD ** -0.5
    to_exp2 = scale * math.log2(math.e)
    place = lax.broadcasted_iota(jnp.int32, (block, 1), 0)
    grad_live = jnp.where(place < own_length, d_out, jnp.zeros_like(d_out))

    def heads(x):
        return [x[:, h * HD:(h + 1) * HD] for h in range(group)]

    query_rows = jnp.concatenate(heads(query), axis=0)
    grad_rows = jnp.concatenate(heads(grad_live), axis=0)
    grad_cols = jnp.concatenate([h.T for h in heads(grad_live)], axis=1)

    scores = lax.dot_general(keys, query_rows, (((1,), (1,)), ((), ())), preferred_element_type=F32)
    row = lax.broadcasted_iota(jnp.int32, (block, block), 1)
    key = lax.broadcasted_iota(jnp.int32, (block, block), 0)
    own_bias = jnp.where((key < own_length) & (key <= row), 0.0, -jnp.inf)
    own_bias = jnp.concatenate([own_bias] * group, axis=1)
    parts = [scores[:prefix_rows], scores[prefix_rows:prefix_rows + block] + own_bias]
    for s, length in enumerate(slot_lengths):
        first = prefix_rows + (s + 1) * block
        parts.append(scores[first:first + block] + jnp.where(place < length, 0.0, -jnp.inf))
    scores = jnp.concatenate(parts, axis=0)
    top = jnp.max(scores, axis=0, keepdims=True) * to_exp2
    exponent = jnp.exp2(scores * to_exp2 - top)
    probs = exponent * (1.0 / jnp.sum(exponent, axis=0, keepdims=True))
    probs_low = probs.astype(BF16)
    attended = lax.dot_general(values, probs_low, (((0,), (0,)), ((), ())), preferred_element_type=F32)
    live = lax.broadcasted_iota(jnp.int32, (1, block), 1) < own_length
    live = jnp.concatenate([jnp.where(live, 1.0, 0.0)] * group, axis=1)
    attended = (attended * live).astype(BF16)
    delta = jnp.sum(grad_cols.astype(F32) * attended.astype(F32), axis=0, keepdims=True)
    grad_probs = jnp.dot(values, grad_cols, preferred_element_type=F32)
    grad_scores = (probs * (grad_probs - delta)).astype(BF16)
    grad_query = lax.dot_general(keys, grad_scores, (((0,), (0,)), ((), ())), preferred_element_type=F32)
    grad_query = (grad_query * scale).astype(BF16)
    grad_keys = jnp.dot(grad_scores, query_rows, preferred_element_type=F32) * scale
    grad_values = jnp.dot(probs_low, grad_rows, preferred_element_type=F32)
    return (
        jnp.concatenate([h.T for h in heads_across(attended, block)], axis=1),
        jnp.concatenate([h.T for h in heads_across(grad_query, block)], axis=1),
        grad_keys,
        grad_values,
    )


def heads_across(x, block):
    return [x[:, h * block:(h + 1) * block] for h in range(x.shape[1] // block)]


def attend_kernel(
    slots, parents, lengths, query, d_out, prefix_k, prefix_v, branch_k, branch_v,
    out, d_query, d_prefix_k, d_prefix_v, d_branch_k, d_branch_v,
):
    me = lax.axis_index("ctx")
    prefix_rows = prefix_k.shape[0]
    block = query.shape[0]
    found = walk_up(parents, lengths, me, slots)
    blocks = [me] + [index for index, _, _ in found]
    keys = jnp.concatenate([prefix_k[...]] + [branch_k[b] for b in blocks], axis=0)
    values = jnp.concatenate([prefix_v[...]] + [branch_v[b] for b in blocks], axis=0)
    out[...], d_query[...], grad_keys, grad_values = attend_group(
        query[...], d_out[...], keys, values, prefix_rows, lengths[0, me], [length for _, length, _ in found]
    )
    for grads, to_prefix, to_branch in ((grad_keys, d_prefix_k, d_branch_k), (grad_values, d_prefix_v, d_branch_v)):
        to_prefix[...] = grads[:prefix_rows]
        to_branch[...] = jnp.zeros_like(to_branch)
        for s, b in enumerate(blocks):
            first = prefix_rows + s * block
            piece = grads[first:first + block]
            if s == 0:
                to_branch[b] = piece
            else:
                @pl.when(found[s - 1][2])
                def _():
                    to_branch[b] = piece


def per_device(query, d_out, branch_kv, prefix_kv, parents, lengths):
    num_blocks = parents.shape[1]
    slots = max(4, num_blocks // 4) - 1
    block = query.shape[1]
    width = query.shape[2]
    with_features = lax.all_gather(prefix_kv, "smp", axis=1, tiled=True)
    prefix_all = lax.all_gather(with_features, "ctx", axis=0, tiled=True)
    prefix_rows, features = prefix_all.shape
    all_blocks = lax.all_gather(branch_kv[0], "ctx", axis=0)
    group_width = width // HK
    smem = pl.BlockSpec(memory_space=pltpu.SMEM)
    heads = pl.BlockSpec((block, group_width), lambda g: (0, g))
    prefix_k = pl.BlockSpec((prefix_rows, HD), lambda g: (0, g))
    prefix_v = pl.BlockSpec((prefix_rows, HD), lambda g: (0, g + HK))
    branch_k = pl.BlockSpec((num_blocks, block, HD), lambda g: (0, 0, g))
    branch_v = pl.BlockSpec((num_blocks, block, HD), lambda g: (0, 0, g + HK))
    grad_prefix = jax.ShapeDtypeStruct((prefix_rows, features // 2), F32)
    grad_branch = jax.ShapeDtypeStruct((num_blocks, block, features // 2), F32)
    out, d_query, dpk, dpv, dbk, dbv = pl.pallas_call(
        functools.partial(attend_kernel, slots),
        grid=(HK,),
        in_specs=[smem, smem, heads, heads, prefix_k, prefix_v, branch_k, branch_v],
        out_specs=[heads, heads, prefix_k, prefix_k, branch_k, branch_k],
        out_shape=[
            jax.ShapeDtypeStruct((block, width), BF16),
            jax.ShapeDtypeStruct((block, width), BF16),
            grad_prefix, grad_prefix, grad_branch, grad_branch,
        ],
        compiler_params=pltpu.CompilerParams(vmem_limit_bytes=56 * 1024 * 1024),
    )(parents, lengths, query[0], d_out[0], prefix_all, prefix_all, all_blocks, all_blocks)
    spread = jnp.concatenate([dbk, dbv], axis=2).reshape(num_blocks * block, features)
    grad_branch = lax.psum_scatter(spread, "ctx", scatter_dimension=0, tiled=True)
    grad_rows = lax.psum_scatter(jnp.concatenate([dpk, dpv], axis=1), "ctx", scatter_dimension=0, tiled=True)
    grad_prefix_out = lax.psum_scatter(grad_rows, "smp", scatter_dimension=1, tiled=True)
    return out[None], d_query[None], grad_branch.astype(BF16)[None], grad_prefix_out.astype(BF16)


def solution(mesh):
    return jax.shard_map(
        per_device,
        mesh=mesh,
        in_specs=(
            P("smp", "ctx", None),
            P("smp", "ctx", None),
            P("smp", "ctx", None),
            P("ctx", "smp"),
            P("smp", None),
            P("smp", None),
        ),
        out_specs=(
            P("smp", "ctx", None),
            P("smp", "ctx", None),
            P("smp", "ctx", None),
            P("ctx", "smp"),
        ),
        check_vma=False,
    )
```

time: 333 us -> 267 us (0.80)
  matrix products: 59.2 us -> 0 us
  local copies, waits for them, and re-layouts: 36.4 us -> 0.01 us
  waiting for transfers between devices: 168 us -> 186 us
  Pallas kernels: 0 us -> 15.6 us
  other arithmetic: 13.6 us -> 9.63 us
    dot_general x33 -> x0, matrix products: 59.2 us -> none  [the longest x4 10.5 us: one_head(): jnp.dot(prob_round, value_head, preferred_element_type=jnp.float32)]
    pallas_call x0 -> x1, Pallas kernels: none -> 15.6 us  [per_device(): pl.pallas_call(functools.partial(attend_kernel, slots), grid=(HK,), in_sp...]
    reduce_scatter x1, waiting for transfers between devices: 6.12 us -> 17 us  [per_device(): lax.psum_scatter(grad_rows, 'smp', scatter_dimension=1, tiled=True)]
    unnamed x20 -> x2, local copies, waits for them, and re-layouts: 8.23 us -> 0.01 us
    dynamic_update_slice x8 -> x0, local copies, waits for them, and re-layouts: 7.37 us -> none  [attend(): lax.map(one_head, (query_heads, grad_heads, key_heads, value_heads))]
    convert_element_type x5 -> x1, other arithmetic: 7.98 us -> 1.37 us  [per_device(): grad_prefix_out.astype(BF16)]
    concatenate x1 -> x2, other arithmetic: 0.1 us -> 6.49 us  [the longest x1 4.05 us: per_device(): jnp.concatenate([dbk, dbv], axis=2).reshape(num_blocks * block, features)]
    slice x4 -> x0, local copies, waits for them, and re-layouts: 5.11 us -> none  [the longest x1 1.73 us: per_device(): grad_pairs[prefix_rows:].reshape(depth_slots, block_rows, feature_count)]
  transfers between devices with their start and end apart: 4 -> 4, of which waited for: 4 -> 4; matrix products, arithmetic and copies ran while one was open for 7% -> 2% of each run, Pallas kernels for 0% -> 0%
where the time goes in v1:
time: 267 us
  waiting for transfers between devices  186 us (70%)
  blocking collectives  41.7 us (16%)
  Pallas kernels  15.6 us (6%)
  between operations  13.8 us (5%)
  other arithmetic  9.63 us (4%)
    reduce_scatter x1, waiting for transfers between devices, per_device(): lax.psum_scatter(spread, 'ctx', scatter_dimension=0, tiled=True)  90.1 us
    reduce_scatter x1, waiting for transfers between devices, per_device(): lax.psum_scatter(jnp.concatenate([dpk, dpv], axis=1), 'ctx', scatter_dime...  63.1 us
    all_gather x1, blocking collectives, per_device(): prefix_all = lax.all_gather(with_features, 'ctx', axis=0, tiled=True)  35.3 us
    reduce_scatter x1, waiting for transfers between devices, per_device(): lax.psum_scatter(grad_rows, 'smp', scatter_dimension=1, tiled=True)  17 us
    pallas_call x1, Pallas kernels, per_device(): pl.pallas_call(functools.partial(attend_kernel, slots), grid=(HK,), in_sp...  15.6 us
    all_gather x1, waiting for transfers between devices, per_device(): all_blocks = lax.all_gather(branch_kv[0], 'ctx', axis=0)  14.8 us
    all_gather x1, blocking collectives, per_device(): with_features = lax.all_gather(prefix_kv, 'smp', axis=1, tiled=True)  6.43 us
  transfers between devices with their start and end apart: 4, of which 4 were waited for; matrix products, arithmetic and copies ran while one was open for 2% of the time, Pallas kernels for 0%

profile of v1, /device:TPU:0, one launch (start us, length us, event | category | flops | bytes accessed | tf_op | source)
XLA Modules:
  0.0 266.7 jit_solution(1556532680190231007)
XLA Ops:
  7.2 0.0 all-gather.2.cloned.1.call-start
  7.2 0.7 all-gather.2.cloned.1.call-update
  7.9 0.0 reduce-scatter.6.cloned.1.call-start
  7.9 6.4 %all_gather.9 = bf16[32,1024]{1,0:T(8,128)(2,1)S(1)} all-gather(bf16[32,256]{1,0:T(8,128)(2,1)} %param.9), channel_id=1, replica_groups=mesh['smp'=4,'ctx'=8] {'smp'}, dimensions={1}, use_global_device_ids=true | all-gather | bytes 81920 | tf_op jit(solution)/shard_map/all_gather | solution.py:113
  14.4 35.3 %all_gather.10.prefix_k.prefix_v = bf16[256,1024]{1,0:T(8,128)(2,1)} all-gather(bf16[32,1024]{1,0:T(8,128)(2,1)S(1)} %all_gather.9), channel_id=1, replica_groups=mesh['smp'=4,'ctx'=8] {'ctx'}, dimensions={0}, use_global_device_ids=true | all-gather | bytes 589824 | tf_op jit(solution)/shard_map/all_gather | solution.py:114
  49.7 14.8 %all-gather.2.cloned.1.call-done.branch_k.branch_v = bf16[8,128,1024]{2,1,0:T(8,128)(2,1)} async-done(((bf16[1,128,1024]{2,1,0:T(8,128)(2,1)}), bf16[8,128,1024]{2,1,0:T(8,128)(2,1)}) %all-gather.2.cloned.1.call-update) | async-done | bytes 2097168 | tf_op jit(solution)/shard_map/all_gather | solution.py:116
  64.5 15.6 %shard_map.93 = (bf16[128,4096]{1,0:T(8,128)(2,1)}, bf16[128,4096]{1,0:T(8,128)(2,1)}, f32[256,512]{1,0:T(8,128)}, f32[256,512]{1,0:T(8,128)}, f32[8,128,512]{2,1,0:T(8,128)}, /*index=5*/f32[8,128,512]{2,1,0:T(8,128)}) custom-call(s32[1,8]{1,0:T(1,128)} %parents.1, s32[1,8]{1,0:T(1,128)} %lengths.1, bf16[128,4096]{1,0:T(8,128)(2,1)} %bitcast.8, ...), custom_call_target="tpu_custom_call" | custom-call | tf_op jit(solution)/shard_map/pallas_call | solution.py:126
  80.1 0.0 copy-start
  80.1 2.4 pad_maximum_fusion.1
  82.6 0.0 reduce-scatter.6.cloned.1.call-update
  82.6 0.0 reduce-scatter.8.cloned.1.call-start
  82.6 63.1 %reduce-scatter.6.cloned.1.call-done = f32[32,1024]{1,0:T(8,128)} async-done(((f32[256,1024]{1,0:T(8,128)}), f32[32,1024]{1,0:T(8,128)}) %reduce-scatter.6.cloned.1.call-update) | async-done | bytes 131088 | tf_op jit(solution)/shard_map/reduce_scatter | solution.py:140
  145.8 0.0 reduce-scatter.8.cloned.1.call-update
  145.8 0.0 reduce-scatter.4.cloned.1.call-start
  145.8 0.0 copy-done
  145.8 4.1 %pad_maximum_fusion = f32[8,128,1024]{2,1,0:T(8,128)} fusion(f32[8,128,512]{2,1,0:T(8,128)} %get-tuple-element.13, f32[8,128,512]{2,1,0:T(8,128)S(1)} %copy-done), kind=kLoop, calls=%fused_computation | loop fusion | flops 1048576 | bytes 8388608 | tf_op jit(solution)/shard_map/concatenate | solution.py:138
  149.9 0.0 reduce-scatter.4.cloned.1.call-update
  149.9 17.0 %reduce-scatter.8.cloned.1.call-done = f32[32,256]{1,0:T(8,128)} async-done(((f32[32,1024]{1,0:T(8,128)}), f32[32,256]{1,0:T(8,128)}) %reduce-scatter.8.cloned.1.call-update) | async-done | bytes 32784 | tf_op jit(solution)/shard_map/reduce_scatter | solution.py:141
  166.9 1.4 convert_element_type.7
  168.3 90.1 %reduce-scatter.4.cloned.1.call-done = f32[128,1024]{1,0:T(8,128)} async-done(((f32[1024,1024]{1,0:T(8,128)}), f32[128,1024]{1,0:T(8,128)}) %reduce-scatter.4.cloned.1.call-update) | async-done | bytes 524304 | tf_op jit(solution)/shard_map/reduce_scatter | solution.py:139
  258.4 1.8 convert_bitcast_fusion
Async XLA Ops:
  7.2 57.3 %all-gather.2.cloned.1.call-start = ((), (), s32[]{:S(2)}) async-start(), calls=%async_computation.3 | async-start | bytes 2359296 | tf_op jit(solution)/shard_map/all_gather | solution.py:116
  7.9 137.9 %reduce-scatter.6.cloned.1.call-start = ((), (), s32[]{:S(2)}) async-start(), calls=%async_computation.5 | async-start | bytes 1179648 | tf_op jit(solution)/shard_map/reduce_scatter | solution.py:140
  80.1 65.7 %copy-start = (f32[8,128,512]{2,1,0:T(8,128)S(1)}, f32[8,128,512]{2,1,0:T(8,128)}, u32[]{:S(2)}) copy-start(f32[8,128,512]{2,1,0:T(8,128)} %get-tuple-element.12) | copy-start | bytes 6291460
  82.6 84.3 %reduce-scatter.8.cloned.1.call-start = ((), (), s32[]{:S(2)}) async-start(), calls=%async_computation.6 | async-start | bytes 163840 | tf_op jit(solution)/shard_map/reduce_scatter | solution.py:141
  145.8 112.6 %reduce-scatter.4.cloned.1.call-start = ((), (), s32[]{:S(2)}) async-start(), calls=%async_computation.4 | async-start | bytes 4718592 | tf_op jit(solution)/shard_map/reduce_scatter | solution.py:139
Sparse Core Ops, SparseCore 0:
  10.1 54.2 all-gather.1
  82.7 63.0 reduce-scatter.5
  148.3 18.5 reduce-scatter.7
  170.4 87.9 reduce-scatter.3

commit v2 on v1

--- a/solution.py
+++ b/solution.py
@@ -105,7 +105,7 @@
                     to_branch[b] = piece
 
 
-def per_device(query, d_out, branch_kv, prefix_kv, parents, lengths):
+def per_device_general(query, d_out, branch_kv, prefix_kv, parents, lengths):
     num_blocks = parents.shape[1]
     slots = max(4, num_blocks // 4) - 1
     block = query.shape[1]
@@ -142,6 +142,410 @@
     return out[None], d_query[None], grad_branch.astype(BF16)[None], grad_prefix_out.astype(BF16)
 
 
+CHUNKS = 4
+SLOTS = 3
+MESH = pl.DeviceIdType.MESH
+VMEM_LIMIT = 56 * 1024 * 1024
+
+
+def greet(ctx_size, smp_size, me, smp):
+    barrier = pltpu.get_barrier_semaphore()
+    for d in range(1, ctx_size):
+        pl.semaphore_signal(barrier, inc=1, device_id={"ctx": lax.rem(me + d, ctx_size)}, device_id_type=MESH)
+    for d in range(1, smp_size):
+        pl.semaphore_signal(barrier, inc=1, device_id={"smp": lax.rem(smp + d, smp_size)}, device_id_type=MESH)
+    pl.semaphore_wait(barrier, ctx_size + smp_size - 2)
+
+
+def remote(src, dst, send, recv, to):
+    return pltpu.make_async_remote_copy(
+        src_ref=src, dst_ref=dst, send_sem=send, recv_sem=recv, device_id=to, device_id_type=MESH
+    )
+
+
+def gather_kernel(
+    ctx_size, smp_size, parents, branch, prefix, blocks, prefix_all,
+    stage, z_send, y_send, recv, p_send, p_recv, q_send, q_recv,
+):
+    me, smp = lax.axis_index("ctx"), lax.axis_index("smp")
+    side = lax.rem(me, 2)
+    beside = me + 1 - 2 * side
+    rows = branch.shape[0] // CHUNKS
+    p_rows, p_cols = prefix.shape
+    greet(ctx_size, smp_size, me, smp)
+
+    def part(c):
+        return pl.ds(c * rows, rows)
+
+    def up(src, k, c):
+        return remote(src, blocks.at[k, part(c)], z_send.at[k, c], recv.at[k, c], {"ctx": me + 2})
+
+    def across(k, c):
+        return remote(branch.at[part(c)], blocks.at[k, part(c)], y_send.at[c], recv.at[k, c], {"ctx": beside})
+
+    def arrived(k, c):
+        across(k, c).wait_recv()
+
+    p_own = (pl.ds(pl.multiple_of(me * p_rows, p_rows), p_rows), pl.ds(pl.multiple_of(smp * p_cols, p_cols), p_cols))
+    q_own = (slice(None), p_own[1])
+
+    def p_copy(d):
+        return remote(prefix, prefix_all.at[p_own], p_send.at[d - 1], p_recv.at[d - 1], {"ctx": lax.rem(me + d, ctx_size)})
+
+    def q_copy(d):
+        return remote(
+            prefix_all.at[q_own], prefix_all.at[q_own], q_send.at[d - 1], q_recv.at[d - 1],
+            {"smp": lax.rem(smp + d, smp_size)},
+        )
+
+    for d in range(1, ctx_size):
+        p_copy(d).start()
+    for device, k in ((0, 0), (1, 1), (2, 2), (4, 3), (5, 3), (6, 3)):
+        @pl.when(me == device)
+        def _():
+            for c in range(CHUNKS):
+                across(k, c).start()
+                if k < 3:
+                    up(branch.at[part(c)], k, c).start()
+    prefix_all[p_own] = prefix[...]
+    for d in range(1, ctx_size):
+        p_copy(d).wait_recv()
+    for d in range(1, smp_size):
+        q_copy(d).start()
+
+    for device, order in ((0, (1,)), (1, (0,)), (2, (0, 1)), (3, (2, 1, 0))):
+        @pl.when(me == device)
+        def _():
+            for c in range(CHUNKS):
+                for k in order:
+                    arrived(k, c)
+                    up(blocks.at[k, part(c)], k, c).start()
+
+    @pl.when((me == 4) | (me == 5))
+    def _():
+        first = parents[0, 6]
+        second = jnp.where(first >= 0, parents[0, jnp.maximum(first, 0)], -1)
+        for c in range(CHUNKS):
+            for k in range(4):
+                arrived(k, c)
+            for k, want in enumerate((first, second)):
+                total = jnp.where(want == me, 1.0, 0.0) * branch[part(c)].astype(F32)
+                for held, index in ((0, 0), (1, 1), (2, 2), (3, beside)):
+                    total += jnp.where(want == index, 1.0, 0.0) * blocks[held, part(c)].astype(F32)
+                stage[k, part(c)] = total.astype(BF16)
+                up(stage.at[k, part(c)], k, c).start()
+
+    @pl.when(me >= 6)
+    def _():
+        for c in range(CHUNKS):
+            for k in range(2):
+                arrived(k, c)
+
+    @pl.when(me == 7)
+    def _():
+        for c in range(CHUNKS):
+            arrived(3, c)
+
+    blocks[4] = branch[...]
+    for d in range(1, smp_size):
+        q_copy(d).wait_recv()
+    for d in range(1, ctx_size):
+        p_copy(d).wait_send()
+    for d in range(1, smp_size):
+        q_copy(d).wait_send()
+
+    @pl.when((me != 3) & (me != 7))
+    def _():
+        for c in range(CHUNKS):
+            across(0, c).wait_send()
+
+    @pl.when(me < 6)
+    def _():
+        for c in range(CHUNKS):
+            for k in range(2):
+                up(blocks.at[k, part(c)], k, c).wait_send()
+
+    @pl.when((me == 2) | (me == 3))
+    def _():
+        for c in range(CHUNKS):
+            up(blocks.at[2, part(c)], 2, c).wait_send()
+
+
+def slot_attend_kernel(
+    parents, lengths, query, d_out, prefix_k, prefix_v, block_k, block_v,
+    out, d_query, d_prefix, d_slots, d_own,
+):
+    me = lax.axis_index("ctx")
+    group = pl.program_id(0)
+    prefix_rows = prefix_k.shape[0]
+    block = query.shape[0]
+    half = d_own.shape[1] // 2
+    found = walk_up(parents, lengths, me, SLOTS)
+    held = []
+    for s, (index, _, _) in enumerate(found):
+        last = 3 if s == 0 else s - 1
+        held.append(jnp.where(me < 6, jnp.minimum(index, 3), jnp.where(me == 6, s, last)))
+    read = [4] + [jnp.where(found[s][2], held[s], 4) for s in range(SLOTS)]
+    keys = jnp.concatenate([prefix_k[...]] + [block_k[b] for b in read], axis=0)
+    values = jnp.concatenate([prefix_v[...]] + [block_v[b] for b in read], axis=0)
+    out[...], d_query[...], grad_keys, grad_values = attend_group(
+        query[...], d_out[...], keys, values, prefix_rows, lengths[0, me], [length for _, length, _ in found]
+    )
+    for grads, offset in ((grad_keys, 0), (grad_values, half)):
+        columns = pl.ds(pl.multiple_of(offset + group * HD, HD), HD)
+        d_prefix[:, columns] = grads[:prefix_rows].astype(BF16)
+        d_own[:, columns] = grads[prefix_rows:prefix_rows + block]
+        d_slots[:, :, columns] = jnp.zeros((4, block, HD), BF16)
+        for s in range(SLOTS):
+            first = prefix_rows + (s + 1) * block
+            piece = grads[first:first + block].astype(BF16)
+
+            @pl.when(found[s][2])
+            def _():
+                d_slots[held[s], :, columns] = piece
+
+
+def reduce_kernel(
+    ctx_size, smp_size, parents, d_slots, d_own, d_prefix, out, out_prefix,
+    below, beside_in, sums, p_in, p_sum, p_low, q_in,
+    z_send, z_recv, y_send, y_recv, p_send, p_recv, q_send, q_recv,
+):
+    me, smp = lax.axis_index("ctx"), lax.axis_index("smp")
+    side = lax.rem(me, 2)
+    beside = me + 1 - 2 * side
+    rows = out.shape[0] // CHUNKS
+    p_rows, p_cols = out_prefix.shape
+    greet(ctx_size, smp_size, me, smp)
+
+    def part(c):
+        return pl.ds(c * rows, rows)
+
+    def down(src, k, c):
+        return remote(src, below.at[k, part(c)], z_send.at[k, c], z_recv.at[k, c], {"ctx": me - 2})
+
+    def across(src, c):
+        return remote(src, beside_in.at[part(c)], y_send.at[c], y_recv.at[c], {"ctx": beside})
+
+    def from_above(k, c):
+        down(sums.at[k, part(c)], k, c).wait_recv()
+
+    def from_beside(c):
+        across(sums.at[3, part(c)], c).wait_recv()
+
+    def p_copy(d):
+        to = lax.rem(smp + d, smp_size)
+        columns = pl.ds(pl.multiple_of(to * p_cols, p_cols), p_cols)
+        return remote(d_prefix.at[:, columns], p_in.at[d - 1], p_send.at[d - 1], p_recv.at[d - 1], {"smp": to})
+
+    def q_copy(d):
+        to = lax.rem(me + d, ctx_size)
+        piece = pl.ds(pl.multiple_of(to * p_rows, p_rows), p_rows)
+        return remote(p_low.at[piece], q_in.at[d - 1], q_send.at[d - 1], q_recv.at[d - 1], {"ctx": to})
+
+    def sum_prefix():
+        columns = pl.ds(pl.multiple_of(smp * p_cols, p_cols), p_cols)
+        for d in range(1, smp_size):
+            p_copy(d).wait_recv()
+        total = d_prefix[:, columns].astype(F32)
+        for d in range(1, smp_size):
+            total += p_in[d - 1].astype(F32)
+        p_sum[...] = total
+        p_low[...] = total.astype(BF16)
+        for d in range(1, ctx_size):
+            q_copy(d).start()
+
+    def load(ref, k, c):
+        return ref[k, part(c)].astype(F32)
+
+    for device in (6, 7):
+        @pl.when(me == device)
+        def _():
+            for c in range(CHUNKS):
+                for k in range(2):
+                    down(d_slots.at[k, part(c)], k, c).start()
+                if device == 7:
+                    across(d_slots.at[3, part(c)], c).start()
+    for d in range(1, smp_size):
+        p_copy(d).start()
+
+    @pl.when((me < 4) | (me >= 6))
+    def _():
+        sum_prefix()
+
+    @pl.when((me == 4) | (me == 5))
+    def _():
+        first = parents[0, 6]
+        second = jnp.where(first >= 0, parents[0, jnp.maximum(first, 0)], -1)
+        for c in range(CHUNKS):
+            from_above(0, c)
+            from_above(1, c)
+            near, far = load(below, 0, c), load(below, 1, c)
+
+            def share(index):
+                return jnp.where(first == index, 1.0, 0.0) * near + jnp.where(second == index, 1.0, 0.0) * far
+
+            for k, index in ((0, 0), (1, 1), (2, 2), (3, beside)):
+                sums[k, part(c)] = (load(d_slots, k, c) + share(index)).astype(BF16)
+                if k < 3:
+                    down(sums.at[k, part(c)], k, c).start()
+                else:
+                    across(sums.at[3, part(c)], c).start()
+        sum_prefix()
+
+    for device in (2, 3):
+        @pl.when(me == device)
+        def _():
+            for c in range(CHUNKS):
+                for k in range(3):
+                    from_above(k, c)
+                    if k < 2 or device == 3:
+                        sums[k, part(c)] = (load(d_slots, k, c) + load(below, k, c)).astype(BF16)
+                    if k < 2:
+                        down(sums.at[k, part(c)], k, c).start()
+                    elif device == 3:
+                        across(sums.at[2, part(c)], c).start()
+
+    for device in (0, 1):
+        @pl.when(me == device)
+        def _():
+            for c in range(CHUNKS):
+                for k in range(2):
+                    from_above(k, c)
+                other = 1 - device
+                sums[3, part(c)] = (load(d_slots, other, c) + load(below, other, c)).astype(BF16)
+                across(sums.at[3, part(c)], c).start()
+
+    for device, slot in ((0, 0), (1, 1), (2, 2), (6, None), (4, None), (5, None)):
+        @pl.when(me == device)
+        def _():
+            for c in range(CHUNKS):
+                from_beside(c)
+                total = beside_in[part(c)].astype(F32)
+                if slot is not None:
+                    total += load(below, slot, c)
+                if device in (4, 5):
+                    first = parents[0, 6]
+                    second = jnp.where(first >= 0, parents[0, jnp.maximum(first, 0)], -1)
+                    total += jnp.where(first == me, 1.0, 0.0) * load(below, 0, c)
+                    total += jnp.where(second == me, 1.0, 0.0) * load(below, 1, c)
+                out[part(c)] = (d_own[part(c)] + total).astype(BF16)
+
+    @pl.when((me == 3) | (me == 7))
+    def _():
+        out[...] = d_own[...].astype(BF16)
+
+    own_rows = pl.ds(pl.multiple_of(me * p_rows, p_rows), p_rows)
+    total = p_sum[own_rows]
+    for d in range(1, ctx_size):
+        q_copy(d).wait_recv()
+        total += q_in[d - 1].astype(F32)
+    out_prefix[...] = total.astype(BF16)
+
+    for d in range(1, smp_size):
+        p_copy(d).wait_send()
+    for d in range(1, ctx_size):
+        q_copy(d).wait_send()
+
+    @pl.when((me != 2) & (me != 6))
+    def _():
+        for c in range(CHUNKS):
+            across(sums.at[3, part(c)], c).wait_send()
+
+    @pl.when(me >= 2)
+    def _():
+        for c in range(CHUNKS):
+            for k in range(2):
+                down(sums.at[k, part(c)], k, c).wait_send()
+
+    @pl.when((me == 4) | (me == 5))
+    def _():
+        for c in range(CHUNKS):
+            down(sums.at[2, part(c)], 2, c).wait_send()
+
+
+def per_device(query, d_out, branch_kv, prefix_kv, parents, lengths):
+    ctx_size, smp_size = lax.axis_size("ctx"), lax.axis_size("smp")
+    if parents.shape[1] != 8 or ctx_size != 8:
+        return per_device_general(query, d_out, branch_kv, prefix_kv, parents, lengths)
+    block, width = query.shape[1:]
+    features = branch_kv.shape[2]
+    p_rows, p_cols = prefix_kv.shape
+    prefix_rows = p_rows * ctx_size
+    group_width = width // HK
+    smem = pl.BlockSpec(memory_space=pltpu.SMEM)
+    vmem = pl.BlockSpec(memory_space=pltpu.VMEM)
+    dma = pltpu.SemaphoreType.DMA
+    blocks, prefix_all = pl.pallas_call(
+        functools.partial(gather_kernel, ctx_size, smp_size),
+        in_specs=[smem, vmem, vmem],
+        out_specs=[vmem, vmem],
+        out_shape=[
+            jax.ShapeDtypeStruct((5, block, features), BF16),
+            jax.ShapeDtypeStruct((prefix_rows, features), BF16),
+        ],
+        scratch_shapes=[
+            pltpu.VMEM((2, block, features), BF16),
+            dma((3, CHUNKS)), dma((CHUNKS,)), dma((4, CHUNKS)),
+            dma((ctx_size - 1,)), dma((ctx_size - 1,)), dma((smp_size - 1,)), dma((smp_size - 1,)),
+        ],
+        compiler_params=pltpu.CompilerParams(
+            collective_id=0, has_side_effects=True, vmem_limit_bytes=VMEM_LIMIT
+        ),
+        name="gather_blocks",
+    )(parents, branch_kv[0], prefix_kv)
+
+    def whole(*shape):
+        return pl.BlockSpec(shape, lambda g: (0,) * len(shape))
+
+    heads = pl.BlockSpec((block, group_width), lambda g: (0, g))
+    out, d_query, d_prefix, d_slots, d_own = pl.pallas_call(
+        slot_attend_kernel,
+        grid=(HK,),
+        in_specs=[
+            smem, smem, heads, heads,
+            pl.BlockSpec((prefix_rows, HD), lambda g: (0, g)),
+            pl.BlockSpec((prefix_rows, HD), lambda g: (0, g + HK)),
+            pl.BlockSpec((5, block, HD), lambda g: (0, 0, g)),
+            pl.BlockSpec((5, block, HD), lambda g: (0, 0, g + HK)),
+        ],
+        out_specs=[heads, heads, whole(prefix_rows, features), whole(4, block, features), whole(block, features)],
+        out_shape=[
+            jax.ShapeDtypeStruct((block, width), BF16),
+            jax.ShapeDtypeStruct((block, width), BF16),
+            jax.ShapeDtypeStruct((prefix_rows, features), BF16),
+            jax.ShapeDtypeStruct((4, block, features), BF16),
+            jax.ShapeDtypeStruct((block, features), F32),
+        ],
+        compiler_params=pltpu.CompilerParams(vmem_limit_bytes=VMEM_LIMIT),
+        name="attend",
+    )(parents, lengths, query[0], d_out[0], prefix_all, prefix_all, blocks, blocks)
+    d_branch, d_prefix_out = pl.pallas_call(
+        functools.partial(reduce_kernel, ctx_size, smp_size),
+        in_specs=[smem, vmem, vmem, vmem],
+        out_specs=[vmem, vmem],
+        out_shape=[
+            jax.ShapeDtypeStruct((block, features), BF16),
+            jax.ShapeDtypeStruct((p_rows, p_cols), BF16),
+        ],
+        scratch_shapes=[
+            pltpu.VMEM((3, block, features), BF16),
+            pltpu.VMEM((block, features), BF16),
+            pltpu.VMEM((4, block, features), BF16),
+            pltpu.VMEM((smp_size - 1, prefix_rows, p_cols), BF16),
+            pltpu.VMEM((prefix_rows, p_cols), F32),
+            pltpu.VMEM((prefix_rows, p_cols), BF16),
+            pltpu.VMEM((ctx_size - 1, p_rows, p_cols), BF16),
+            dma((3, CHUNKS)), dma((3, CHUNKS)), dma((CHUNKS,)), dma((CHUNKS,)),
+            dma((smp_size - 1,)), dma((smp_size - 1,)), dma((ctx_size - 1,)), dma((ctx_size - 1,)),
+        ],
+        compiler_params=pltpu.CompilerParams(
+            collective_id=1, has_side_effects=True, vmem_limit_bytes=VMEM_LIMIT
+        ),
+        name="reduce_grads",
+    )(parents, d_slots, d_own, d_prefix)
+    return out[None], d_query[None], d_branch[None], d_prefix_out
+
+
 def solution(mesh):
     return jax.shard_map(
         per_device,

time: 267 us -> 93.2 us (0.35)
  waiting for transfers between devices: 186 us -> 0 us
  Pallas kernels: 15.6 us -> 89.2 us
  blocking collectives: 41.7 us -> 0 us
  between operations: 13.8 us -> 0.65 us
  other arithmetic: 9.63 us -> 0 us
  local copies, waits for them, and re-layouts: 0.01 us -> 2.99 us
    reduce_scatter x3 -> x0, waiting for transfers between devices: 170 us -> none  [the longest x1 90.1 us: per_device(): lax.psum_scatter(spread, 'ctx', scatter_dimension=0, tiled=True)]
    pallas_call x1 -> x3, Pallas kernels: 15.6 us -> 89.2 us  [the longest x1 51.4 us: per_device(): pl.pallas_call(functools.partial(reduce_kernel, ctx_size, smp_size), in_s...]
    all_gather x2 -> x0, blocking collectives: 41.7 us -> none  [the longest x1 35.3 us: per_device(): prefix_all = lax.all_gather(with_features, 'ctx', axis=0, tiled=True)]
    all_gather x1 -> x0, waiting for transfers between devices: 14.8 us -> none  [per_device(): all_blocks = lax.all_gather(branch_kv[0], 'ctx', axis=0)]
    concatenate x2 -> x0, other arithmetic: 6.49 us -> none  [the longest x1 4.05 us: per_device(): jnp.concatenate([dbk, dbv], axis=2).reshape(num_blocks * block, features)]
    unnamed x2, local copies, waits for them, and re-layouts: 0.01 us -> 2.99 us
  transfers between devices with their start and end apart: 4 -> 0, of which waited for: 4 -> 0; matrix products, arithmetic and copies ran while one was open for 2% -> 0% of each run, Pallas kernels for 0% -> 0%
where the time goes in v2:
time: 93.2 us; the launch traced here: 92.9 us
  Pallas kernels  89.2 us (96%)
  local copies, waits for them, and re-layouts  2.99 us (3%)
    pallas_call x1, Pallas kernels, per_device(): pl.pallas_call(functools.partial(reduce_kernel, ctx_size, smp_size), in_s...  51.4 us
    pallas_call x1, Pallas kernels, per_device(): pl.pallas_call(functools.partial(gather_kernel, ctx_size, smp_size), in_s...  22 us
    pallas_call x1, Pallas kernels, per_device(): pl.pallas_call(slot_attend_kernel, grid=(HK,), in_specs=[smem, smem, head...  15.9 us
    unnamed x2, local copies, waits for them, and re-layouts  2.99 us

profile of v2, /device:TPU:0, one launch (start us, length us, event | category | flops | bytes accessed | tf_op | source)
XLA Modules:
  0.0 92.9 jit_solution(1150173609555314386)
XLA Ops:
  0.6 22.0 %gather_blocks.1 = (bf16[5,128,1024]{2,1,0:T(8,128)(2,1)}, bf16[256,1024]{1,0:T(8,128)(2,1)}) custom-call(s32[1,8]{1,0:T(1,128)} %parents.5, bf16[128,1024]{1,0:T(8,128)(2,1)} %bitcast.8, bf16[32,256]{1,0:T(8,128)(2,1)} %prefix.1), custom_call_target="tpu_custom_call" | custom-call | tf_op jit(solution)/shard_map/gather_blocks/pallas_call | solution.py:478
  22.7 15.9 %attend.1 = (bf16[128,4096]{1,0:T(8,128)(2,1)}, bf16[128,4096]{1,0:T(8,128)(2,1)}, bf16[256,1024]{1,0:T(8,128)(2,1)}, bf16[4,128,1024]{2,1,0:T(8,128)(2,1)}, f32[128,1024]{1,0:T(8,128)}) custom-call(s32[1,8]{1,0:T(1,128)} %parents.5, s32[1,8]{1,0:T(1,128)} %lengths.1, bf16[128,4096]{1,0:T(8,128)(2,1)} %bitcast.6, bf16[128,4096]{1,0:T(8,128)(2,1)} %bitcast.7, ...), custom_call_target="tpu_custom_call" | custom-call | tf_op jit(solution)/shard_map/attend/pallas_call | solution.py:501
  38.5 51.4 %reduce_grads.1 = (bf16[128,1024]{1,0:T(8,128)(2,1)}, bf16[32,256]{1,0:T(8,128)(2,1)}) custom-call(s32[1,8]{1,0:T(1,128)} %parents.5, bf16[4,128,1024]{2,1,0:T(8,128)(2,1)} %get-tuple-element.17.d_slots, f32[128,1024]{1,0:T(8,128)} %get-tuple-element.18.d_own, bf16[256,1024]{1,0:T(8,128)(2,1)} %get-tuple-element.19.d_prefix), custom_call_target="tpu_custom_call" | custom-call | tf_op jit(solution)/shard_map/reduce_grads/pallas_call | solution.py:522
  89.9 1.7 %copy.12 = bf16[1,128,1024]{2,1,0:T(8,128)(2,1)} copy(bf16[1,128,1024]{2,1,0:T(8,128)(2,1)} %bitcast.9) | data formatting | bytes 524288
  91.5 1.3 %copy.13 = bf16[32,256]{1,0:T(8,128)(2,1)} copy(bf16[32,256]{1,0:T(8,128)(2,1)} %get-tuple-element.29) | data formatting | bytes 32768

commit v3 on v1

--- a/solution.py
+++ b/solution.py
@@ -105,7 +105,7 @@
                     to_branch[b] = piece
 
 
-def per_device(query, d_out, branch_kv, prefix_kv, parents, lengths):
+def per_device_general(query, d_out, branch_kv, prefix_kv, parents, lengths):
     num_blocks = parents.shape[1]
     slots = max(4, num_blocks // 4) - 1
     block = query.shape[1]
@@ -142,6 +142,361 @@
     return out[None], d_query[None], grad_branch.astype(BF16)[None], grad_prefix_out.astype(BF16)
 
 
+SLOTS = 3
+MESH = pl.DeviceIdType.MESH
+VMEM_LIMIT = 56 * 1024 * 1024
+
+
+def greet(ctx_size, smp_size, me, smp):
+    barrier = pltpu.get_barrier_semaphore()
+    for d in range(1, ctx_size):
+        pl.semaphore_signal(barrier, inc=1, device_id={"ctx": lax.rem(me + d, ctx_size)}, device_id_type=MESH)
+    for d in range(1, smp_size):
+        pl.semaphore_signal(barrier, inc=1, device_id={"smp": lax.rem(smp + d, smp_size)}, device_id_type=MESH)
+    pl.semaphore_wait(barrier, ctx_size + smp_size - 2)
+
+
+def remote(src, dst, send, recv, to):
+    return pltpu.make_async_remote_copy(
+        src_ref=src, dst_ref=dst, send_sem=send, recv_sem=recv, device_id=to, device_id_type=MESH
+    )
+
+
+def tree_kernel(
+    ctx_size, smp_size, parents, lengths, query, d_out, branch, prefix,
+    out, d_query, d_branch, d_prefix,
+    own, held, stage, pre_own, pre, mine, d_own, sums, below, beside_in, d_pre, p_in, p_sum, p_low, q_in,
+    up_send, up_recv, over_send, a_send, a_recv, b_send, b_recv,
+    down_send, down_recv, back_send, back_recv, p_send, p_recv, q_send, q_recv,
+):
+    me, smp = lax.axis_index("ctx"), lax.axis_index("smp")
+    beside = me + 1 - 2 * lax.rem(me, 2)
+    block = branch.shape[0]
+    group_width = query.shape[1] // HK
+    p_rows = prefix.shape[0]
+    prefix_rows = pre.shape[1]
+    greet(ctx_size, smp_size, me, smp)
+
+    def up(src, k, c):
+        return remote(src, held.at[c, k], up_send.at[k, c], up_recv.at[k, c], {"ctx": me + 2})
+
+    def over(k, c):
+        return remote(own.at[c], held.at[c, k], over_send.at[c], up_recv.at[k, c], {"ctx": beside})
+
+    def arrived(k, c):
+        over(k, c).wait_recv()
+
+    def down(k, c):
+        return remote(sums.at[c, k], below.at[c, k], down_send.at[k, c], down_recv.at[k, c], {"ctx": me - 2})
+
+    def back(k, c):
+        return remote(sums.at[c, k], beside_in.at[c], back_send.at[c], back_recv.at[c], {"ctx": beside})
+
+    my_rows = pl.ds(pl.multiple_of(me * p_rows, p_rows), p_rows)
+    my_columns = pl.ds(2 * smp, 2)
+
+    def a_copy(d):
+        return remote(
+            pre_own, pre.at[my_columns, my_rows], a_send.at[d - 1], a_recv.at[d - 1], {"ctx": lax.rem(me + d, ctx_size)}
+        )
+
+    def b_copy(d):
+        return remote(
+            pre.at[my_columns], pre.at[my_columns], b_send.at[d - 1], b_recv.at[d - 1],
+            {"smp": lax.rem(smp + d, smp_size)},
+        )
+
+    def p_copy(d):
+        to = lax.rem(smp + d, smp_size)
+        return remote(d_pre.at[pl.ds(2 * to, 2)], p_in.at[d - 1], p_send.at[d - 1], p_recv.at[d - 1], {"smp": to})
+
+    def q_copy(d):
+        to = lax.rem(me + d, ctx_size)
+        rows = pl.ds(pl.multiple_of(to * p_rows, p_rows), p_rows)
+        return remote(p_low.at[:, rows], q_in.at[d - 1], q_send.at[d - 1], q_recv.at[d - 1], {"ctx": to})
+
+    for i in range(2):
+        pre_own[i] = prefix[:, i * HD:(i + 1) * HD]
+        pre[2 * smp + i, my_rows] = prefix[:, i * HD:(i + 1) * HD]
+    for d in range(1, ctx_size):
+        a_copy(d).start()
+    for c in range(HK):
+        own[c, 0] = branch[:, c * HD:(c + 1) * HD]
+        own[c, 1] = branch[:, (HK + c) * HD:(HK + c + 1) * HD]
+    for device, k in ((0, 0), (1, 1), (2, 2), (4, 3), (5, 3), (6, 3)):
+        @pl.when(me == device)
+        def _():
+            for c in range(HK):
+                over(k, c).start()
+                if k < 3 and c < 2:
+                    up(own.at[c], k, c).start()
+    for k, without in ((0, me == 0), (1, me == 1), (2, (me < 3) | (me > 5)), (3, (me < 4) | (me == 6))):
+        @pl.when(without)
+        def _():
+            for c in range(HK):
+                held[c, k] = jnp.zeros(held.shape[2:], BF16)
+    for d in range(1, ctx_size):
+        a_copy(d).wait_recv()
+    for d in range(1, smp_size):
+        b_copy(d).start()
+
+    first = parents[0, 6]
+    second = jnp.where(first >= 0, parents[0, jnp.maximum(first, 0)], -1)
+    found = walk_up(parents, lengths, me, SLOTS)
+    weight = []
+    for s, (index, _, there) in enumerate(found):
+        place = jnp.where(me < 6, jnp.minimum(index, 3), jnp.where(me == 6, s, 3 if s == 0 else s - 1))
+        weight.append([jnp.where(there & (place == k), 1.0, 0.0) for k in range(4)])
+
+    def forward(c):
+        for device, order in ((0, (1,)), (1, (0,)), (2, (0, 1)), (3, (2, 1, 0))):
+            @pl.when(me == device)
+            def _():
+                for k in order:
+                    arrived(k, c)
+                    up(held.at[c, k], k, c).start()
+                if device < 3:
+                    @pl.when(c < HK - 2)
+                    def _():
+                        up(own.at[c + 2], device, c + 2).start()
+
+        @pl.when((me == 4) | (me == 5))
+        def _():
+            for k in range(4):
+                arrived(k, c)
+            for k, want in enumerate((first, second)):
+                total = jnp.where(want == me, 1.0, 0.0) * own[c].astype(F32)
+                for slot, index in ((0, 0), (1, 1), (2, 2), (3, beside)):
+                    total += jnp.where(want == index, 1.0, 0.0) * held[c, slot].astype(F32)
+                stage[c, k] = total.astype(BF16)
+                up(stage.at[c, k], k, c).start()
+
+        @pl.when(me >= 6)
+        def _():
+            for k in range(2):
+                arrived(k, c)
+
+        @pl.when(me == 7)
+        def _():
+            arrived(3, c)
+
+    def compute(c):
+        sides = []
+        for i in range(2):
+            parts = [pre[HK * i + c], own[c, i]]
+            slots = [held[c, k, i].astype(F32) for k in range(4)]
+            for w in weight:
+                parts.append((w[0] * slots[0] + w[1] * slots[1] + w[2] * slots[2] + w[3] * slots[3]).astype(BF16))
+            sides.append(jnp.concatenate(parts, axis=0))
+        columns = pl.ds(pl.multiple_of(c * group_width, group_width), group_width)
+        out[:, columns], d_query[:, columns], grad_keys, grad_values = attend_group(
+            query[:, columns], d_out[:, columns], sides[0], sides[1], prefix_rows, lengths[0, me],
+            [length for _, length, _ in found],
+        )
+        for i, grads in enumerate((grad_keys, grad_values)):
+            d_pre[HK * i + c] = grads[:prefix_rows].astype(BF16)
+            d_own[c, i] = grads[prefix_rows:prefix_rows + block]
+            pieces = [grads[prefix_rows + s * block:prefix_rows + (s + 1) * block] for s in range(1, SLOTS + 1)]
+            for k in range(4):
+                mine[c, k, i] = weight[0][k] * pieces[0] + weight[1][k] * pieces[1] + weight[2][k] * pieces[2]
+
+        @pl.when(me >= 6)
+        def _():
+            for k in range(2):
+                sums[c, k] = mine[c, k].astype(BF16)
+                down(k, c).start()
+
+        @pl.when(me == 7)
+        def _():
+            sums[c, 3] = mine[c, 3].astype(BF16)
+            back(3, c).start()
+
+    def shared(c, index):
+        near, far = below[c, 0].astype(F32), below[c, 1].astype(F32)
+        return jnp.where(first == index, 1.0, 0.0) * near + jnp.where(second == index, 1.0, 0.0) * far
+
+    def add_down(c):
+        @pl.when((me == 4) | (me == 5))
+        def _():
+            for k in range(2):
+                down(k, c).wait_recv()
+            for k, index in ((0, 0), (1, 1), (2, 2), (3, beside)):
+                sums[c, k] = (mine[c, k] + shared(c, index)).astype(BF16)
+                if k < 3:
+                    down(k, c).start()
+                else:
+                    back(3, c).start()
+
+        for device in (2, 3):
+            @pl.when(me == device)
+            def _():
+                for k in range(3):
+                    down(k, c).wait_recv()
+                    if k < 2 or device == 3:
+                        sums[c, k] = (mine[c, k] + below[c, k].astype(F32)).astype(BF16)
+                    if k < 2:
+                        down(k, c).start()
+                    elif device == 3:
+                        back(2, c).start()
+
+        for device in (0, 1):
+            @pl.when(me == device)
+            def _():
+                for k in range(2):
+                    down(k, c).wait_recv()
+                sums[c, 3] = (mine[c, 1 - device] + below[c, 1 - device].astype(F32)).astype(BF16)
+                back(3, c).start()
+
+    def sum_prefix():
+        for d in range(1, smp_size):
+            p_copy(d).wait_recv()
+        total = d_pre[my_columns].astype(F32)
+        for d in range(1, smp_size):
+            total += p_in[d - 1].astype(F32)
+        p_sum[...] = total
+        p_low[...] = total.astype(BF16)
+        for d in range(1, ctx_size):
+            q_copy(d).start()
+
+    lag = jnp.where(me >= 6, 0, 1)
+    down_lag = jnp.where(me >= 4, 3, 4)
+    prefix_step = jnp.where(me >= 6, HK + 1, jnp.where(me >= 4, HK + 3, HK + 2))
+
+    @pl.loop(0, 2 * HK)
+    def _(t):
+        @pl.when(t < HK)
+        def _():
+            forward(t)
+
+        @pl.when(t == 0)
+        def _():
+            for d in range(1, smp_size):
+                b_copy(d).wait_recv()
+
+        @pl.when((t >= lag) & (t < HK + lag))
+        def _():
+            compute(t - lag)
+
+        @pl.when(t == HK)
+        def _():
+            for d in range(1, smp_size):
+                p_copy(d).start()
+
+        @pl.when(t == prefix_step)
+        def _():
+            sum_prefix()
+
+        @pl.when((t >= down_lag) & (t < HK + down_lag) & (me < 6))
+        def _():
+            add_down(t - down_lag)
+
+    for device in (0, 1, 2, 4, 5, 6):
+        @pl.when(me == device)
+        def _():
+            for c in range(HK):
+                back(3, c).wait_recv()
+                total = d_own[c] + beside_in[c].astype(F32)
+                if device < 3:
+                    total += below[c, device].astype(F32)
+                elif device < 6:
+                    total += shared(c, me)
+                for i in range(2):
+                    d_branch[:, (HK * i + c) * HD:(HK * i + c + 1) * HD] = total[i].astype(BF16)
+
+    @pl.when((me == 3) | (me == 7))
+    def _():
+        for c in range(HK):
+            for i in range(2):
+                d_branch[:, (HK * i + c) * HD:(HK * i + c + 1) * HD] = d_own[c, i].astype(BF16)
+
+    total = p_sum[:, my_rows]
+    for d in range(1, ctx_size):
+        q_copy(d).wait_recv()
+        total += q_in[d - 1].astype(F32)
+    for i in range(2):
+        d_prefix[:, i * HD:(i + 1) * HD] = total[i].astype(BF16)
+
+    for d in range(1, ctx_size):
+        a_copy(d).wait_send()
+        q_copy(d).wait_send()
+    for d in range(1, smp_size):
+        b_copy(d).wait_send()
+        p_copy(d).wait_send()
+
+    def drain(active, copy, slots):
+        @pl.when(active)
+        def _():
+            for c in range(HK):
+                for k in slots:
+                    copy(k, c).wait_send()
+
+    def climb(k, c):
+        return up(held.at[c, k], k, c)
+
+    drain((me != 3) & (me != 7), over, (0,))
+    drain(me < 6, climb, (0, 1))
+    drain((me == 2) | (me == 3), climb, (2,))
+    drain((me != 2) & (me != 6), back, (3,))
+    drain(me >= 2, down, (0, 1))
+    drain((me == 4) | (me == 5), down, (2,))
+
+
+def remote(src, dst, send, recv, to):
+    return pltpu.make_async_remote_copy(
+        src_ref=src, dst_ref=dst, send_sem=send, recv_sem=recv, device_id=to, device_id_type=MESH
+    )
+
+
+def per_device(query, d_out, branch_kv, prefix_kv, parents, lengths):
+    ctx_size, smp_size = lax.axis_size("ctx"), lax.axis_size("smp")
+    p_rows, p_cols = prefix_kv.shape
+    if parents.shape[1] != 8 or ctx_size != 8 or p_cols != 2 * HD:
+        return per_device_general(query, d_out, branch_kv, prefix_kv, parents, lengths)
+    block, width = query.shape[1:]
+    prefix_rows = p_rows * ctx_size
+    smem = pl.BlockSpec(memory_space=pltpu.SMEM)
+    vmem = pl.BlockSpec(memory_space=pltpu.VMEM)
+    dma = pltpu.SemaphoreType.DMA
+    pair = (2, block, HD)
+    out, d_query, d_branch, d_prefix = pl.pallas_call(
+        functools.partial(tree_kernel, ctx_size, smp_size),
+        in_specs=[smem, smem, vmem, vmem, vmem, vmem],
+        out_specs=[vmem] * 4,
+        out_shape=[
+            jax.ShapeDtypeStruct((block, width), BF16),
+            jax.ShapeDtypeStruct((block, width), BF16),
+            jax.ShapeDtypeStruct(branch_kv.shape[1:], BF16),
+            jax.ShapeDtypeStruct(prefix_kv.shape, BF16),
+        ],
+        scratch_shapes=[
+            pltpu.VMEM((HK,) + pair, BF16),
+            pltpu.VMEM((HK, 4) + pair, BF16),
+            pltpu.VMEM((HK, 2) + pair, BF16),
+            pltpu.VMEM((2, p_rows, HD), BF16),
+            pltpu.VMEM((2 * HK, prefix_rows, HD), BF16),
+            pltpu.VMEM((HK, 4) + pair, F32),
+            pltpu.VMEM((HK,) + pair, F32),
+            pltpu.VMEM((HK, 4) + pair, BF16),
+            pltpu.VMEM((HK, 3) + pair, BF16),
+            pltpu.VMEM((HK,) + pair, BF16),
+            pltpu.VMEM((2 * HK, prefix_rows, HD), BF16),
+            pltpu.VMEM((smp_size - 1, 2, prefix_rows, HD), BF16),
+            pltpu.VMEM((2, prefix_rows, HD), F32),
+            pltpu.VMEM((2, prefix_rows, HD), BF16),
+            pltpu.VMEM((ctx_size - 1, 2, p_rows, HD), BF16),
+            dma((3, HK)), dma((4, HK)), dma((HK,)),
+            dma((ctx_size - 1,)), dma((ctx_size - 1,)), dma((smp_size - 1,)), dma((smp_size - 1,)),
+            dma((3, HK)), dma((3, HK)), dma((HK,)), dma((HK,)),
+            dma((smp_size - 1,)), dma((smp_size - 1,)), dma((ctx_size - 1,)), dma((ctx_size - 1,)),
+        ],
+        compiler_params=pltpu.CompilerParams(
+            collective_id=0, has_side_effects=True, vmem_limit_bytes=VMEM_LIMIT
+        ),
+        name="tree_attention",
+    )(parents, lengths, query[0], d_out[0], branch_kv[0], prefix_kv)
+    return out[None], d_query[None], d_branch[None], d_prefix
+
+
 def solution(mesh):
     return jax.shard_map(
         per_device,

time: 267 us -> 72.1 us (0.27)
  waiting for transfers between devices: 186 us -> 0 us
  Pallas kernels: 15.6 us -> 66.4 us
  blocking collectives: 41.7 us -> 0 us
  between operations: 13.8 us -> 0.65 us
  other arithmetic: 9.63 us -> 0 us
  local copies, waits for them, and re-layouts: 0.01 us -> 4.79 us
    reduce_scatter x3 -> x0, waiting for transfers between devices: 170 us -> none  [the longest x1 90.1 us: per_device(): lax.psum_scatter(spread, 'ctx', scatter_dimension=0, tiled=True)]
    pallas_call x1, Pallas kernels: 15.6 us -> 66.4 us  [per_device(): pl.pallas_call(functools.partial(tree_kernel, ctx_size, smp_size), in_spe...]
    all_gather x2 -> x0, blocking collectives: 41.7 us -> none  [the longest x1 35.3 us: per_device(): prefix_all = lax.all_gather(with_features, 'ctx', axis=0, tiled=True)]
    all_gather x1 -> x0, waiting for transfers between devices: 14.8 us -> none  [per_device(): all_blocks = lax.all_gather(branch_kv[0], 'ctx', axis=0)]
    concatenate x2 -> x0, other arithmetic: 6.49 us -> none  [the longest x1 4.05 us: per_device(): jnp.concatenate([dbk, dbv], axis=2).reshape(num_blocks * block, features)]
    unnamed x2 -> x10, local copies, waits for them, and re-layouts: 0.01 us -> 4.79 us
  transfers between devices with their start and end apart: 4 -> 0, of which waited for: 4 -> 0; matrix products, arithmetic and copies ran while one was open for 2% -> 0% of each run, Pallas kernels for 0% -> 0%
where the time goes in v3:
time: 72.1 us; the launch traced here: 71.8 us
  Pallas kernels  66.4 us (92%)
  local copies, waits for them, and re-layouts  4.79 us (7%)
    pallas_call x1, Pallas kernels, per_device(): pl.pallas_call(functools.partial(tree_kernel, ctx_size, smp_size), in_spe...  66.4 us
    unnamed x10, local copies, waits for them, and re-layouts  4.79 us

profile of v3, /device:TPU:0, one launch (start us, length us, event | category | flops | bytes accessed | tf_op | source)
XLA Modules:
  0.0 71.8 jit_solution(13860682644903147756)
XLA Ops:
  0.6 66.4 %tree_attention.1 = (bf16[128,4096]{1,0:T(8,128)(2,1)}, bf16[128,4096]{1,0:T(8,128)(2,1)}, bf16[128,1024]{1,0:T(8,128)(2,1)}, bf16[32,256]{1,0:T(8,128)(2,1)}) custom-call(s32[1,8]{1,0:T(1,128)} %parents.1, s32[1,8]{1,0:T(1,128)} %lengths.1, bf16[128,4096]{1,0:T(8,128)(2,1)} %bitcast.6, bf16[128,4096]{1,0:T(8,128)(2,1)} %bitcast.7, ...), custom_call_target="tpu_custom_call" | custom-call | tf_op jit(solution)/shard_map/tree_attention/pallas_call | solution.py:461
  67.0 0.0 copy-start
  67.0 2.4 %copy.14 = bf16[1,128,4096]{2,1,0:T(8,128)(2,1)} copy(bf16[1,128,4096]{2,1,0:T(8,128)(2,1)} %bitcast.9) | data formatting | bytes 2097152
  69.4 0.0 copy-done
  69.4 0.0 copy-start.1
  69.4 1.0 %copy.15 = bf16[1,128,4096]{2,1,0:T(8,128)(2,1)} copy(bf16[1,128,4096]{2,1,0:T(8,128)(2,1)S(1)} %bitcast.8) | data formatting | bytes 2097152
  70.4 0.1 copy-done.1
  70.5 0.0 copy-start.2
  70.5 0.7 copy.16
  71.2 0.0 copy-done.2
  71.2 0.6 copy.17
Async XLA Ops:
  67.0 2.4 %copy-start = (bf16[128,4096]{1,0:T(8,128)(2,1)S(1)}, bf16[128,4096]{1,0:T(8,128)(2,1)}, u32[]{:S(2)}) copy-start(bf16[128,4096]{1,0:T(8,128)(2,1)} %get-tuple-element.9) | copy-start | bytes 3145732
  69.4 1.1 %copy-start.1 = (bf16[128,1024]{1,0:T(8,128)(2,1)S(1)}, bf16[128,1024]{1,0:T(8,128)(2,1)}, u32[]{:S(2)}) copy-start(bf16[128,1024]{1,0:T(8,128)(2,1)} %get-tuple-element.10) | copy-start | bytes 786436
  70.5 0.7 copy-start.2

commit v4 on v3

--- a/solution.py
+++ b/solution.py
@@ -165,12 +165,14 @@
 def tree_kernel(
     ctx_size, smp_size, parents, lengths, query, d_out, branch, prefix,
     out, d_query, d_branch, d_prefix,
-    own, held, stage, pre_own, pre, mine, d_own, sums, below, beside_in, d_pre, p_in, p_sum, p_low, q_in,
-    up_send, up_recv, over_send, a_send, a_recv, b_send, b_recv,
-    down_send, down_recv, back_send, back_recv, p_send, p_recv, q_send, q_recv,
+    own, held, stage, pre_own, pre, mine, d_own, other, sums, to_beside, below, other_in, beside_in,
+    d_pre, p_in, p_sum, p_low, q_in,
+    up_send, up_recv, over_send, over_recv, aside_send, aside_recv, a_send, a_recv, b_send, b_recv,
+    down_send, down_recv, cross_send, cross_recv, back_send, back_recv, p_send, p_recv, q_send, q_recv,
 ):
     me, smp = lax.axis_index("ctx"), lax.axis_index("smp")
-    beside = me + 1 - 2 * lax.rem(me, 2)
+    side = lax.rem(me, 2)
+    beside = me + 1 - 2 * side
     block = branch.shape[0]
     group_width = query.shape[1] // HK
     p_rows = prefix.shape[0]
@@ -178,19 +180,29 @@
     greet(ctx_size, smp_size, me, smp)
 
     def up(src, k, c):
-        return remote(src, held.at[c, k], up_send.at[k, c], up_recv.at[k, c], {"ctx": me + 2})
+        return remote(src, held.at[c, k, side], up_send.at[k, c], up_recv.at[k, c], {"ctx": me + 2})
+
+    def aside(k, c):
+        half = held.at[c, k, side]
+        return remote(half, half, aside_send.at[k, c], aside_recv.at[k, c], {"ctx": beside})
 
     def over(k, c):
-        return remote(own.at[c], held.at[c, k], over_send.at[c], up_recv.at[k, c], {"ctx": beside})
-
-    def arrived(k, c):
-        over(k, c).wait_recv()
+        return remote(own.at[c], held.at[c, k], over_send.at[c], over_recv.at[c], {"ctx": beside})
+
+    def over_keys(k, c):
+        return remote(own.at[c, 0], held.at[c, k, 0], over_send.at[c], over_recv.at[c], {"ctx": beside})
 
     def down(k, c):
         return remote(sums.at[c, k], below.at[c, k], down_send.at[k, c], down_recv.at[k, c], {"ctx": me - 2})
 
-    def back(k, c):
-        return remote(sums.at[c, k], beside_in.at[c], back_send.at[c], back_recv.at[c], {"ctx": beside})
+    def cross(k, c):
+        return remote(other.at[c, k], other_in.at[c, k], cross_send.at[k, c], cross_recv.at[k, c], {"ctx": beside})
+
+    def back(c):
+        return remote(to_beside.at[c], beside_in.at[c], back_send.at[c], back_recv.at[c], {"ctx": beside})
+
+    def back_keys(c):
+        return remote(to_beside.at[c, 0], beside_in.at[c, 0], back_send.at[c], back_recv.at[c], {"ctx": beside})
 
     my_rows = pl.ds(pl.multiple_of(me * p_rows, p_rows), p_rows)
     my_columns = pl.ds(2 * smp, 2)
@@ -227,14 +239,19 @@
         @pl.when(me == device)
         def _():
             for c in range(HK):
-                over(k, c).start()
+                (over_keys if device in (1, 5) else over)(k, c).start()
                 if k < 3 and c < 2:
-                    up(own.at[c], k, c).start()
+                    up(own.at[c, device % 2], k, c).start()
+    for k, without in ((0, me == 0), (1, me < 2), (2, (me < 3) | (me > 5)), (3, (me < 5) | (me == 6))):
+        @pl.when(without)
+        def _():
+            for c in range(HK):
+                held[c, k, 1] = jnp.zeros((block, HD), BF16)
     for k, without in ((0, me == 0), (1, me == 1), (2, (me < 3) | (me > 5)), (3, (me < 4) | (me == 6))):
         @pl.when(without)
         def _():
             for c in range(HK):
-                held[c, k] = jnp.zeros(held.shape[2:], BF16)
+                held[c, k, 0] = jnp.zeros((block, HD), BF16)
     for d in range(1, ctx_size):
         a_copy(d).wait_recv()
     for d in range(1, smp_size):
@@ -249,36 +266,83 @@
         weight.append([jnp.where(there & (place == k), 1.0, 0.0) for k in range(4)])
 
     def forward(c):
-        for device, order in ((0, (1,)), (1, (0,)), (2, (0, 1)), (3, (2, 1, 0))):
-            @pl.when(me == device)
+        def pass_on(k):
+            up(held.at[c, k, side], k, c).wait_recv()
+            up(held.at[c, k, side], k, c).start()
+            aside(k, c).start()
+
+        def next_own(device):
+            @pl.when(c < HK - 2)
             def _():
-                for k in order:
-                    arrived(k, c)
-                    up(held.at[c, k], k, c).start()
-                if device < 3:
-                    @pl.when(c < HK - 2)
-                    def _():
-                        up(own.at[c + 2], device, c + 2).start()
+                up(own.at[c + 2, device % 2], device, c + 2).start()
+
+        @pl.when(me == 0)
+        def _():
+            over_keys(1, c).wait_recv()
+            up(held.at[c, 1, 0], 1, c).start()
+            next_own(0)
+
+        @pl.when(me == 1)
+        def _():
+            over(0, c).wait_recv()
+            up(held.at[c, 0, 1], 0, c).start()
+            next_own(1)
+
+        @pl.when(me == 2)
+        def _():
+            pass_on(0)
+            pass_on(1)
+            next_own(2)
+
+        @pl.when(me == 3)
+        def _():
+            over(2, c).wait_recv()
+            up(held.at[c, 2, 1], 2, c).start()
+            pass_on(1)
+            pass_on(0)
 
         @pl.when((me == 4) | (me == 5))
         def _():
-            for k in range(4):
-                arrived(k, c)
+            for k in range(3):
+                up(held.at[c, k, side], k, c).wait_recv()
+                aside(k, c).start()
+
+        @pl.when(me == 4)
+        def _():
+            over_keys(3, c).wait_recv()
+
+        @pl.when(me == 5)
+        def _():
+            over(3, c).wait_recv()
+
+        @pl.when((me == 4) | (me == 5))
+        def _():
             for k, want in enumerate((first, second)):
-                total = jnp.where(want == me, 1.0, 0.0) * own[c].astype(F32)
+                total = jnp.where(want == me, 1.0, 0.0) * own[c, side].astype(F32)
                 for slot, index in ((0, 0), (1, 1), (2, 2), (3, beside)):
-                    total += jnp.where(want == index, 1.0, 0.0) * held[c, slot].astype(F32)
+                    total += jnp.where(want == index, 1.0, 0.0) * held[c, slot, side].astype(F32)
                 stage[c, k] = total.astype(BF16)
                 up(stage.at[c, k], k, c).start()
 
         @pl.when(me >= 6)
         def _():
             for k in range(2):
-                arrived(k, c)
+                up(held.at[c, k, side], k, c).wait_recv()
+                aside(k, c).start()
 
         @pl.when(me == 7)
         def _():
-            arrived(3, c)
+            over(3, c).wait_recv()
+
+    def settle(c):
+        @pl.when(me >= 2)
+        def _():
+            for k in range(2):
+                aside(k, c).wait_recv()
+
+        @pl.when((me == 4) | (me == 5))
+        def _():
+            aside(2, c).wait_recv()
 
     def compute(c):
         sides = []
@@ -300,52 +364,86 @@
             for k in range(4):
                 mine[c, k, i] = weight[0][k] * pieces[0] + weight[1][k] * pieces[1] + weight[2][k] * pieces[2]
 
-        @pl.when(me >= 6)
+        @pl.when(me >= 2)
         def _():
             for k in range(2):
-                sums[c, k] = mine[c, k].astype(BF16)
-                down(k, c).start()
+                other[c, k] = mine[c, k, 1 - side].astype(BF16)
+                cross(k, c).start()
+
+        @pl.when((me == 4) | (me == 5))
+        def _():
+            other[c, 2] = mine[c, 2, 1 - side].astype(BF16)
+            cross(2, c).start()
 
         @pl.when(me == 7)
         def _():
-            sums[c, 3] = mine[c, 3].astype(BF16)
-            back(3, c).start()
+            to_beside[c] = mine[c, 3].astype(BF16)
+            back(c).start()
 
     def shared(c, index):
         near, far = below[c, 0].astype(F32), below[c, 1].astype(F32)
         return jnp.where(first == index, 1.0, 0.0) * near + jnp.where(second == index, 1.0, 0.0) * far
 
     def add_down(c):
+        def send_sum(k, more):
+            cross(k, c).wait_recv()
+            total = mine[c, k, side] + other_in[c, k].astype(F32)
+            if more is not None:
+                total += more
+            sums[c, k] = total.astype(BF16)
+            down(k, c).start()
+
+        @pl.when(me >= 6)
+        def _():
+            for k in range(2):
+                send_sum(k, None)
+
         @pl.when((me == 4) | (me == 5))
         def _():
             for k in range(2):
                 down(k, c).wait_recv()
-            for k, index in ((0, 0), (1, 1), (2, 2), (3, beside)):
-                sums[c, k] = (mine[c, k] + shared(c, index)).astype(BF16)
-                if k < 3:
-                    down(k, c).start()
-                else:
-                    back(3, c).start()
-
-        for device in (2, 3):
-            @pl.when(me == device)
-            def _():
-                for k in range(3):
-                    down(k, c).wait_recv()
-                    if k < 2 or device == 3:
-                        sums[c, k] = (mine[c, k] + below[c, k].astype(F32)).astype(BF16)
-                    if k < 2:
-                        down(k, c).start()
-                    elif device == 3:
-                        back(2, c).start()
-
-        for device in (0, 1):
-            @pl.when(me == device)
-            def _():
-                for k in range(2):
-                    down(k, c).wait_recv()
-                sums[c, 3] = (mine[c, 1 - device] + below[c, 1 - device].astype(F32)).astype(BF16)
-                back(3, c).start()
+            for k in range(3):
+                send_sum(k, shared(c, k))
+
+        @pl.when(me == 4)
+        def _():
+            to_beside[c, 0] = (mine[c, 3, 0] + shared(c, 5)).astype(BF16)
+            back_keys(c).start()
+
+        @pl.when(me == 5)
+        def _():
+            to_beside[c, 0] = mine[c, 3, 0].astype(BF16)
+            to_beside[c, 1] = (mine[c, 3, 1] + shared(c, 4)).astype(BF16)
+            back(c).start()
+
+        @pl.when((me == 2) | (me == 3))
+        def _():
+            for k in range(2):
+                down(k, c).wait_recv()
+                send_sum(k, below[c, k].astype(F32))
+            down(2, c).wait_recv()
+
+        @pl.when(me == 3)
+        def _():
+            to_beside[c, 0] = mine[c, 2, 0].astype(BF16)
+            to_beside[c, 1] = (mine[c, 2, 1] + below[c, 2].astype(F32)).astype(BF16)
+            back(c).start()
+
+        @pl.when(me < 2)
+        def _():
+            for k in range(2):
+                down(k, c).wait_recv()
+
+        @pl.when(me == 0)
+        def _():
+            to_beside[c, 0] = (mine[c, 1, 0] + below[c, 1].astype(F32)).astype(BF16)
+            back_keys(c).start()
+
+        @pl.when(me == 1)
+        def _():
+            to_beside[c, 0] = mine[c, 0, 0].astype(BF16)
+            to_beside[c, 1] = (mine[c, 0, 1] + below[c, 0].astype(F32)).astype(BF16)
+            back(c).start()
 
     def sum_prefix():
         for d in range(1, smp_size):
@@ -358,9 +456,8 @@
         for d in range(1, ctx_size):
             q_copy(d).start()
 
-    lag = jnp.where(me >= 6, 0, 1)
-    down_lag = jnp.where(me >= 4, 3, 4)
-    prefix_step = jnp.where(me >= 6, HK + 1, jnp.where(me >= 4, HK + 3, HK + 2))
+    down_lag = jnp.where(me >= 6, 2, jnp.where(me >= 4, 3, 4))
+    prefix_step = jnp.where(me >= 6, HK + 2, jnp.where(me >= 4, HK + 3, HK + 2))
 
     @pl.loop(0, 2 * HK)
     def _(t):
@@ -373,9 +470,10 @@
             for d in range(1, smp_size):
                 b_copy(d).wait_recv()
 
-        @pl.when((t >= lag) & (t < HK + lag))
-        def _():
-            compute(t - lag)
+        @pl.when((t >= 1) & (t < HK + 1))
+        def _():
+            settle(t - 1)
+            compute(t - 1)
 
         @pl.when(t == HK)
         def _():
@@ -386,7 +484,7 @@
         def _():
             sum_prefix()
 
-        @pl.when((t >= down_lag) & (t < HK + down_lag) & (me < 6))
+        @pl.when((t >= down_lag) & (t < HK + down_lag))
         def _():
             add_down(t - down_lag)
 
@@ -394,14 +492,19 @@
         @pl.when(me == device)
         def _():
             for c in range(HK):
-                back(3, c).wait_recv()
-                total = d_own[c] + beside_in[c].astype(F32)
-                if device < 3:
-                    total += below[c, device].astype(F32)
-                elif device < 6:
-                    total += shared(c, me)
+                if device in (1, 5):
+                    back_keys(c).wait_recv()
+                else:
+                    back(c).wait_recv()
                 for i in range(2):
-                    d_branch[:, (HK * i + c) * HD:(HK * i + c + 1) * HD] = total[i].astype(BF16)
+                    total = d_own[c, i]
+                    if i == 0 or device not in (1, 5):
+                        total += beside_in[c, i].astype(F32)
+                    if i == device % 2 and device < 3:
+                        total += below[c, device].astype(F32)
+                    elif i == device % 2 and device < 6:
+                        total += shared(c, device)
+                    d_branch[:, (HK * i + c) * HD:(HK * i + c + 1) * HD] = total.astype(BF16)
 
     @pl.when((me == 3) | (me == 7))
     def _():
@@ -423,28 +526,39 @@
         b_copy(d).wait_send()
         p_copy(d).wait_send()
 
-    def drain(active, copy, slots):
+    def drain(active, copies):
         @pl.when(active)
         def _():
             for c in range(HK):
-                for k in slots:
-                    copy(k, c).wait_send()
-
-    def climb(k, c):
-        return up(held.at[c, k], k, c)
-
-    drain((me != 3) & (me != 7), over, (0,))
-    drain(me < 6, climb, (0, 1))
-    drain((me == 2) | (me == 3), climb, (2,))
-    drain((me != 2) & (me != 6), back, (3,))
-    drain(me >= 2, down, (0, 1))
-    drain((me == 4) | (me == 5), down, (2,))
-
-
-def remote(src, dst, send, recv, to):
-    return pltpu.make_async_remote_copy(
-        src_ref=src, dst_ref=dst, send_sem=send, recv_sem=recv, device_id=to, device_id_type=MESH
-    )
+                for copy in copies:
+                    copy(c).wait_send()
+
+    def on(copy, k):
+        return lambda c: copy(k, c)
+
+    def climb(k):
+        return lambda c: up(stage.at[c, 0], k, c)
+
+    even = (me == 0) | (me == 2) | (me == 4) | (me == 6)
+    drain(even, (on(over, 0),))
+    drain((me == 1) | (me == 5), (on(over_keys, 1),))
+    drain(me < 6, (climb(0), climb(1)))
+    drain((me == 2) | (me == 3), (climb(2),))
+    drain(me >= 2, (on(aside, 0), on(aside, 1), on(cross, 0), on(cross, 1), on(down, 0), on(down, 1)))
+    drain((me == 4) | (me == 5), (on(aside, 2), on(cross, 2), on(down, 2)))
+    drain(side == 1, (back,))
+    drain((me == 0) | (me == 4), (back_keys,))
+
+
+def hand_over_kernel(a, b, c, d, a_out, b_out, c_out, d_out, sem):
+    copies = [
+        pltpu.make_async_copy(src, dst, sem.at[i])
+        for i, (src, dst) in enumerate(((a, a_out), (b, b_out), (c, c_out), (d, d_out)))
+    ]
+    for copy in copies:
+        copy.start()
+    for copy in copies:
+        copy.wait()
 
 
 def per_device(query, d_out, branch_kv, prefix_kv, parents, lengths):
@@ -457,8 +571,9 @@
     smem = pl.BlockSpec(memory_space=pltpu.SMEM)
     vmem = pl.BlockSpec(memory_space=pltpu.VMEM)
     dma = pltpu.SemaphoreType.DMA
-    pair = (2, block, HD)
-    out, d_query, d_branch, d_prefix = pl.pallas_call(
+    half = (block, HD)
+    pair = (2,) + half
+    results = pl.pallas_call(
         functools.partial(tree_kernel, ctx_size, smp_size),
         in_specs=[smem, smem, vmem, vmem, vmem, vmem],
         out_specs=[vmem] * 4,
@@ -471,22 +586,25 @@
         scratch_shapes=[
             pltpu.VMEM((HK,) + pair, BF16),
             pltpu.VMEM((HK, 4) + pair, BF16),
-            pltpu.VMEM((HK, 2) + pair, BF16),
+            pltpu.VMEM((HK, 2) + half, BF16),
             pltpu.VMEM((2, p_rows, HD), BF16),
             pltpu.VMEM((2 * HK, prefix_rows, HD), BF16),
             pltpu.VMEM((HK, 4) + pair, F32),
             pltpu.VMEM((HK,) + pair, F32),
-            pltpu.VMEM((HK, 4) + pair, BF16),
-            pltpu.VMEM((HK, 3) + pair, BF16),
+            pltpu.VMEM((HK, 3) + half, BF16),
+            pltpu.VMEM((HK, 3) + half, BF16),
+            pltpu.VMEM((HK,) + pair, BF16),
+            pltpu.VMEM((HK, 3) + half, BF16),
+            pltpu.VMEM((HK, 3) + half, BF16),
             pltpu.VMEM((HK,) + pair, BF16),
             pltpu.VMEM((2 * HK, prefix_rows, HD), BF16),
             pltpu.VMEM((smp_size - 1, 2, prefix_rows, HD), BF16),
             pltpu.VMEM((2, prefix_rows, HD), F32),
             pltpu.VMEM((2, prefix_rows, HD), BF16),
             pltpu.VMEM((ctx_size - 1, 2, p_rows, HD), BF16),
-            dma((3, HK)), dma((4, HK)), dma((HK,)),
+            dma((3, HK)), dma((3, HK)), dma((HK,)), dma((HK,)), dma((3, HK)), dma((3, HK)),
             dma((ctx_size - 1,)), dma((ctx_size - 1,)), dma((smp_size - 1,)), dma((smp_size - 1,)),
-            dma((3, HK)), dma((3, HK)), dma((HK,)), dma((HK,)),
+            dma((3, HK)), dma((3, HK)), dma((3, HK)), dma((3, HK)), dma((HK,)), dma((HK,)),
             dma((smp_size - 1,)), dma((smp_size - 1,)), dma((ctx_size - 1,)), dma((ctx_size - 1,)),
         ],
         compiler_params=pltpu.CompilerParams(
@@ -494,6 +612,15 @@
         ),
         name="tree_attention",
     )(parents, lengths, query[0], d_out[0], branch_kv[0], prefix_kv)
+    anywhere = pl.BlockSpec(memory_space=pl.ANY)
+    out, d_query, d_branch, d_prefix = pl.pallas_call(
+        hand_over_kernel,
+        in_specs=[anywhere] * 4,
+        out_specs=[anywhere] * 4,
+        out_shape=[jax.ShapeDtypeStruct(x.shape, x.dtype) for x in results],
+        scratch_shapes=[dma((4,))],
+        name="hand_over",
+    )(*results)
     return out[None], d_query[None], d_branch[None], d_prefix
 
 

time: 72.1 us -> 137 us (1.90)
  Pallas kernels: 66.4 us -> 136 us
  local copies, waits for them, and re-layouts: 4.79 us -> 0 us
    pallas_call x0 -> x1, Pallas kernels: none -> 73.1 us  [per_device(): pl.pallas_call(hand_over_kernel, in_specs=[anywhere] * 4, out_specs=[anyw...]
    unnamed x10 -> x0, local copies, waits for them, and re-layouts: 4.79 us -> none
    pallas_call x1, Pallas kernels: 66.4 us -> 62.8 us  [per_device(): pl.pallas_call(functools.partial(tree_kernel, ctx_size, smp_size), in_spe...]
where the time goes in v4:
time: 137 us
  Pallas kernels  136 us (99%)
    pallas_call x1, Pallas kernels, per_device(): pl.pallas_call(hand_over_kernel, in_specs=[anywhere] * 4, out_specs=[anyw...  73.1 us
    pallas_call x1, Pallas kernels, per_device(): pl.pallas_call(functools.partial(tree_kernel, ctx_size, smp_size), in_spe...  62.8 us

profile of v4, /device:TPU:0, one launch (start us, length us, event | category | flops | bytes accessed | tf_op | source)
XLA Modules:
  0.0 136.5 jit_solution(12960801856573740345)
XLA Ops:
  0.6 62.8 %tree_attention.1 = (bf16[128,4096]{1,0:T(8,128)(2,1)}, bf16[128,4096]{1,0:T(8,128)(2,1)}, bf16[128,1024]{1,0:T(8,128)(2,1)}, bf16[32,256]{1,0:T(8,128)(2,1)}) custom-call(s32[1,8]{1,0:T(1,128)} %parents.1, s32[1,8]{1,0:T(1,128)} %lengths.1, bf16[128,4096]{1,0:T(8,128)(2,1)} %bitcast.6, bf16[128,4096]{1,0:T(8,128)(2,1)} %bitcast.7, ...), custom_call_target="tpu_custom_call" | custom-call | tf_op jit(solution)/shard_map/tree_attention/pallas_call | solution.py:576
  63.4 73.1 %hand_over.1 = (bf16[128,4096]{1,0:T(8,128)(2,1)}, bf16[128,4096]{1,0:T(8,128)(2,1)}, bf16[128,1024]{1,0:T(8,128)(2,1)}, bf16[32,256]{1,0:T(8,128)(2,1)}) custom-call(bf16[128,4096]{1,0:T(8,128)(2,1)} %get-tuple-element.12.a, bf16[128,4096]{1,0:T(8,128)(2,1)} %get-tuple-element.13.b, bf16[128,1024]{1,0:T(8,128)(2,1)} %get-tuple-element.14.c, ...), custom_call_target="tpu_custom_call" | custom-call | tf_op jit(solution)/shard_map/hand_over/pallas_call | solution.py:616

commit v5 on v4

--- a/solution.py
+++ b/solution.py
@@ -162,9 +162,17 @@
     )
 
 
+HEAD_ORDER = (0, 2, 1, 3)
+
+
+def block_columns(i):
+    return slice(i * HD, (i + 1) * HD)
+
+
 def tree_kernel(
-    ctx_size, smp_size, parents, lengths, query, d_out, branch, prefix,
-    out, d_query, d_branch, d_prefix,
+    ctx_size, smp_size, parents, lengths, query_far, d_out_far, branch, prefix,
+    out_far, d_query_far, d_branch, d_prefix,
+    query, d_out, out, d_query, load_sem, store_sem,
     own, held, stage, pre_own, pre, mine, d_own, other, sums, to_beside, below, other_in, beside_in,
     d_pre, p_in, p_sum, p_low, q_in,
     up_send, up_recv, over_send, over_recv, aside_send, aside_recv, a_send, a_recv, b_send, b_recv,
@@ -177,6 +185,11 @@
     group_width = query.shape[1] // HK
     p_rows = prefix.shape[0]
     prefix_rows = pre.shape[1]
+    loads = [
+        pltpu.make_async_copy(query_far, query, load_sem.at[0]), pltpu.make_async_copy(d_out_far, d_out, load_sem.at[1])
+    ]
+    for load in loads:
+        load.start()
     greet(ctx_size, smp_size, me, smp)
 
     def up(src, k, c):
@@ -212,15 +225,28 @@
             pre_own, pre.at[my_columns, my_rows], a_send.at[d - 1], a_recv.at[d - 1], {"ctx": lax.rem(me + d, ctx_size)}
         )
 
-    def b_copy(d):
+    def b_copy(d, i):
+        columns = pre.at[2 * smp + i]
+        return remote(columns, columns, b_send.at[d - 1, i], b_recv.at[d - 1, i], {"smp": lax.rem(smp + d, smp_size)})
+
+    def p_copy(to, d, i):
         return remote(
-            pre.at[my_columns], pre.at[my_columns], b_send.at[d - 1], b_recv.at[d - 1],
-            {"smp": lax.rem(smp + d, smp_size)},
+            d_pre.at[2 * to + i], p_in.at[d - 1, i], p_send.at[d - 1, i], p_recv.at[d - 1, i], {"smp": to}
         )
 
-    def p_copy(d):
-        to = lax.rem(smp + d, smp_size)
-        return remote(d_pre.at[pl.ds(2 * to, 2)], p_in.at[d - 1], p_send.at[d - 1], p_recv.at[d - 1], {"smp": to})
+    def p_after(d, i):
+        return p_copy(lax.rem(smp + d, smp_size), d, i)
+
+    def head_columns(c):
+        head = 2 * lax.rem(c, 2) + lax.div(c, 2)
+        return pl.ds(pl.multiple_of(head * group_width, group_width), group_width)
+
+    def stores(c):
+        columns = head_columns(c)
+        return [
+            pltpu.make_async_copy(src.at[:, columns], dst.at[:, columns], store_sem.at[i, c])
+            for i, (src, dst) in enumerate(((out, out_far), (d_query, d_query_far)))
+        ]
 
     def q_copy(d):
         to = lax.rem(me + d, ctx_size)
@@ -233,14 +259,14 @@
     for d in range(1, ctx_size):
         a_copy(d).start()
     for c in range(HK):
-        own[c, 0] = branch[:, c * HD:(c + 1) * HD]
-        own[c, 1] = branch[:, (HK + c) * HD:(HK + c + 1) * HD]
+        for i in range(2):
+            own[c, i] = branch[:, block_columns(HK * i + HEAD_ORDER[c])]
     for device, k in ((0, 0), (1, 1), (2, 2), (4, 3), (5, 3), (6, 3)):
         @pl.when(me == device)
         def _():
-            for c in range(HK):
+            for c in range(2):
                 (over_keys if device in (1, 5) else over)(k, c).start()
-                if k < 3 and c < 2:
+                if k < 3:
                     up(own.at[c, device % 2], k, c).start()
     for k, without in ((0, me == 0), (1, me < 2), (2, (me < 3) | (me > 5)), (3, (me < 5) | (me == 6))):
         @pl.when(without)
@@ -254,8 +280,9 @@
                 held[c, k, 0] = jnp.zeros((block, HD), BF16)
     for d in range(1, ctx_size):
         a_copy(d).wait_recv()
-    for d in range(1, smp_size):
-        b_copy(d).start()
+    for i in range(2):
+        for d in range(1, smp_size):
+            b_copy(d, i).start()
 
     first = parents[0, 6]
     second = jnp.where(first >= 0, parents[0, jnp.maximum(first, 0)], -1)
@@ -271,28 +298,20 @@
             up(held.at[c, k, side], k, c).start()
             aside(k, c).start()
 
-        def next_own(device):
-            @pl.when(c < HK - 2)
-            def _():
-                up(own.at[c + 2, device % 2], device, c + 2).start()
-
         @pl.when(me == 0)
         def _():
             over_keys(1, c).wait_recv()
             up(held.at[c, 1, 0], 1, c).start()
-            next_own(0)
 
         @pl.when(me == 1)
         def _():
             over(0, c).wait_recv()
             up(held.at[c, 0, 1], 0, c).start()
-            next_own(1)
 
         @pl.when(me == 2)
         def _():
             pass_on(0)
             pass_on(1)
-            next_own(2)
 
         @pl.when(me == 3)
         def _():
@@ -334,6 +353,13 @@
         def _():
             over(3, c).wait_recv()
 
+        for device, k in ((0, 0), (1, 1), (2, 2), (4, 3), (5, 3), (6, 3)):
+            @pl.when((me == device) & (c < HK - 2))
+            def _():
+                (over_keys if device in (1, 5) else over)(k, c + 2).start()
+                if k < 3:
+                    up(own.at[c + 2, device % 2], k, c + 2).start()
+
     def settle(c):
         @pl.when(me >= 2)
         def _():
@@ -346,24 +372,28 @@
 
     def compute(c):
         sides = []
+        head = 2 * lax.rem(c, 2) + lax.div(c, 2)
         for i in range(2):
-            parts = [pre[HK * i + c], own[c, i]]
+            parts = [pre[HK * i + head], own[c, i]]
             slots = [held[c, k, i].astype(F32) for k in range(4)]
             for w in weight:
                 parts.append((w[0] * slots[0] + w[1] * slots[1] + w[2] * slots[2] + w[3] * slots[3]).astype(BF16))
             sides.append(jnp.concatenate(parts, axis=0))
-        columns = pl.ds(pl.multiple_of(c * group_width, group_width), group_width)
+        columns = head_columns(c)
         out[:, columns], d_query[:, columns], grad_keys, grad_values = attend_group(
             query[:, columns], d_out[:, columns], sides[0], sides[1], prefix_rows, lengths[0, me],
             [length for _, length, _ in found],
         )
         for i, grads in enumerate((grad_keys, grad_values)):
-            d_pre[HK * i + c] = grads[:prefix_rows].astype(BF16)
+            d_pre[HK * i + head] = grads[:prefix_rows].astype(BF16)
             d_own[c, i] = grads[prefix_rows:prefix_rows + block]
             pieces = [grads[prefix_rows + s * block:prefix_rows + (s + 1) * block] for s in range(1, SLOTS + 1)]
             for k in range(4):
                 mine[c, k, i] = weight[0][k] * pieces[0] + weight[1][k] * pieces[1] + weight[2][k] * pieces[2]
 
+        for store in stores(c):
+            store.start()
+
         @pl.when(me >= 2)
         def _():
             for k in range(2):
@@ -379,6 +409,13 @@
         def _():
             to_beside[c] = mine[c, 3].astype(BF16)
             back(c).start()
+
+        for i in range(2):
+            to = 2 * i + lax.rem(c, 2)
+
+            @pl.when(smp != to)
+            def _():
+                p_copy(to, lax.rem(to - smp + 4, 4), lax.div(c, 2)).start()
 
     def shared(c, index):
         near, far = below[c, 0].astype(F32), below[c, 1].astype(F32)
@@ -447,7 +484,8 @@
 
     def sum_prefix():
         for d in range(1, smp_size):
-            p_copy(d).wait_recv()
+            for i in range(2):
+                p_after(d, i).wait_recv()
         total = d_pre[my_columns].astype(F32)
         for d in range(1, smp_size):
             total += p_in[d - 1].astype(F32)
@@ -457,7 +495,7 @@
             q_copy(d).start()
 
     down_lag = jnp.where(me >= 6, 2, jnp.where(me >= 4, 3, 4))
-    prefix_step = jnp.where(me >= 6, HK + 2, jnp.where(me >= 4, HK + 3, HK + 2))
+    prefix_step = jnp.where((me >= 4) & (me < 6), HK + 2, HK + 1)
 
     @pl.loop(0, 2 * HK)
     def _(t):
@@ -465,28 +503,30 @@
         def _():
             forward(t)
 
-        @pl.when(t == 0)
-        def _():
+        @pl.when(t == 1)
+        def _():
+            for load in loads:
+                load.wait()
             for d in range(1, smp_size):
-                b_copy(d).wait_recv()
+                b_copy(d, 0).wait_recv()
+
+        @pl.when(t == 3)
+        def _():
+            for d in range(1, smp_size):
+                b_copy(d, 1).wait_recv()
 
         @pl.when((t >= 1) & (t < HK + 1))
         def _():
             settle(t - 1)
             compute(t - 1)
 
-        @pl.when(t == HK)
-        def _():
-            for d in range(1, smp_size):
-                p_copy(d).start()
+        @pl.when((t >= down_lag) & (t < HK + down_lag))
+        def _():
+            add_down(t - down_lag)
 
         @pl.when(t == prefix_step)
         def _():
             sum_prefix()
-
-        @pl.when((t >= down_lag) & (t < HK + down_lag))
-        def _():
-            add_down(t - down_lag)
 
     for device in (0, 1, 2, 4, 5, 6):
         @pl.when(me == device)
@@ -504,13 +544,13 @@
                         total += below[c, device].astype(F32)
                     elif i == device % 2 and device < 6:
                         total += shared(c, device)
-                    d_branch[:, (HK * i + c) * HD:(HK * i + c + 1) * HD] = total.astype(BF16)
+                    d_branch[:, block_columns(HK * i + HEAD_ORDER[c])] = total.astype(BF16)
 
     @pl.when((me == 3) | (me == 7))
     def _():
         for c in range(HK):
             for i in range(2):
-                d_branch[:, (HK * i + c) * HD:(HK * i + c + 1) * HD] = d_own[c, i].astype(BF16)
+                d_branch[:, block_columns(HK * i + HEAD_ORDER[c])] = d_own[c, i].astype(BF16)
 
     total = p_sum[:, my_rows]
     for d in range(1, ctx_size):
@@ -523,8 +563,12 @@
         a_copy(d).wait_send()
         q_copy(d).wait_send()
     for d in range(1, smp_size):
-        b_copy(d).wait_send()
-        p_copy(d).wait_send()
+        for i in range(2):
+            b_copy(d, i).wait_send()
+            p_after(d, i).wait_send()
+    for c in range(HK):
+        for store in stores(c):
+            store.wait()
 
     def drain(active, copies):
         @pl.when(active)
@@ -550,33 +594,28 @@
     drain((me == 0) | (me == 4), (back_keys,))
 
 
-def hand_over_kernel(a, b, c, d, a_out, b_out, c_out, d_out, sem):
-    copies = [
-        pltpu.make_async_copy(src, dst, sem.at[i])
-        for i, (src, dst) in enumerate(((a, a_out), (b, b_out), (c, c_out), (d, d_out)))
-    ]
-    for copy in copies:
-        copy.start()
-    for copy in copies:
-        copy.wait()
+def hand_over_kernel(a, b, c, d, a_out, b_out, c_out, d_out):
+    for src, dst in ((a, a_out), (b, b_out), (c, c_out), (d, d_out)):
+        dst[...] = src[...]
 
 
 def per_device(query, d_out, branch_kv, prefix_kv, parents, lengths):
     ctx_size, smp_size = lax.axis_size("ctx"), lax.axis_size("smp")
     p_rows, p_cols = prefix_kv.shape
-    if parents.shape[1] != 8 or ctx_size != 8 or p_cols != 2 * HD:
+    if parents.shape[1] != 8 or ctx_size != 8 or p_cols != 2 * HD or smp_size != 4:
         return per_device_general(query, d_out, branch_kv, prefix_kv, parents, lengths)
     block, width = query.shape[1:]
     prefix_rows = p_rows * ctx_size
     smem = pl.BlockSpec(memory_space=pltpu.SMEM)
     vmem = pl.BlockSpec(memory_space=pltpu.VMEM)
     dma = pltpu.SemaphoreType.DMA
+    anywhere = pl.BlockSpec(memory_space=pl.ANY)
     half = (block, HD)
     pair = (2,) + half
     results = pl.pallas_call(
         functools.partial(tree_kernel, ctx_size, smp_size),
-        in_specs=[smem, smem, vmem, vmem, vmem, vmem],
-        out_specs=[vmem] * 4,
+        in_specs=[smem, smem, anywhere, anywhere, vmem, vmem],
+        out_specs=[anywhere, anywhere, vmem, vmem],
         out_shape=[
             jax.ShapeDtypeStruct((block, width), BF16),
             jax.ShapeDtypeStruct((block, width), BF16),
@@ -584,6 +623,11 @@
             jax.ShapeDtypeStruct(prefix_kv.shape, BF16),
         ],
         scratch_shapes=[
+            pltpu.VMEM((block, width), BF16),
+            pltpu.VMEM((block, width), BF16),
+            pltpu.VMEM((block, width), BF16),
+            pltpu.VMEM((block, width), BF16),
+            dma((2,)), dma((2, HK)),
             pltpu.VMEM((HK,) + pair, BF16),
             pltpu.VMEM((HK, 4) + pair, BF16),
             pltpu.VMEM((HK, 2) + half, BF16),
@@ -603,22 +647,23 @@
             pltpu.VMEM((2, prefix_rows, HD), BF16),
             pltpu.VMEM((ctx_size - 1, 2, p_rows, HD), BF16),
             dma((3, HK)), dma((3, HK)), dma((HK,)), dma((HK,)), dma((3, HK)), dma((3, HK)),
-            dma((ctx_size - 1,)), dma((ctx_size - 1,)), dma((smp_size - 1,)), dma((smp_size - 1,)),
+            dma((ctx_size - 1,)), dma((ctx_size - 1,)), dma((smp_size - 1, 2)), dma((smp_size - 1, 2)),
             dma((3, HK)), dma((3, HK)), dma((3, HK)), dma((3, HK)), dma((HK,)), dma((HK,)),
-            dma((smp_size - 1,)), dma((smp_size - 1,)), dma((ctx_size - 1,)), dma((ctx_size - 1,)),
+            dma((smp_size - 1, 2)), dma((smp_size - 1, 2)), dma((ctx_size - 1,)), dma((ctx_size - 1,)),
         ],
         compiler_params=pltpu.CompilerParams(
             collective_id=0, has_side_effects=True, vmem_limit_bytes=VMEM_LIMIT
         ),
         name="tree_attention",
     )(parents, lengths, query[0], d_out[0], branch_kv[0], prefix_kv)
-    anywhere = pl.BlockSpec(memory_space=pl.ANY)
+    rows = [pl.BlockSpec((x.shape[0] // HK, x.shape[1]), lambda r: (r, 0)) for x in results[:3]]
+    rows.append(pl.BlockSpec(results[3].shape, lambda r: (0, 0)))
     out, d_query, d_branch, d_prefix = pl.pallas_call(
         hand_over_kernel,
-        in_specs=[anywhere] * 4,
-        out_specs=[anywhere] * 4,
+        grid=(HK,),
+        in_specs=rows,
+        out_specs=rows,
         out_shape=[jax.ShapeDtypeStruct(x.shape, x.dtype) for x in results],
-        scratch_shapes=[dma((4,))],
         name="hand_over",
     )(*results)
     return out[None], d_query[None], d_branch[None], d_prefix

time: 137 us -> 61.9 us (0.45)
  Pallas kernels: 136 us -> 61.1 us
    pallas_call x1, Pallas kernels: 73.1 us -> 3.83 us  [per_device(): pl.pallas_call(hand_over_kernel, grid=(HK,), in_specs=rows, out_specs=row...]
    pallas_call x1, Pallas kernels: 62.8 us -> 57.3 us  [per_device(): pl.pallas_call(functools.partial(tree_kernel, ctx_size, smp_size), in_spe...]
where the time goes in v5:
time: 61.9 us; the launch traced here: 61.7 us
  Pallas kernels  61.1 us (99%)
  between operations  0.64 us (1%)
    pallas_call x1, Pallas kernels, per_device(): pl.pallas_call(functools.partial(tree_kernel, ctx_size, smp_size), in_spe...  57.3 us
    pallas_call x1, Pallas kernels, per_device(): pl.pallas_call(hand_over_kernel, grid=(HK,), in_specs=rows, out_specs=row...  3.83 us

profile of v5, /device:TPU:0, one launch (start us, length us, event | category | flops | bytes accessed | tf_op | source)
XLA Modules:
  0.0 61.7 jit_solution(13916747095779745508)
XLA Ops:
  0.6 57.3 %tree_attention.1 = (bf16[128,4096]{1,0:T(8,128)(2,1)}, bf16[128,4096]{1,0:T(8,128)(2,1)}, bf16[128,1024]{1,0:T(8,128)(2,1)}, bf16[32,256]{1,0:T(8,128)(2,1)}) custom-call(s32[1,8]{1,0:T(1,128)} %parents.1, s32[1,8]{1,0:T(1,128)} %lengths.1, bf16[128,4096]{1,0:T(8,128)(2,1)} %bitcast.6, bf16[128,4096]{1,0:T(8,128)(2,1)} %bitcast.7, ...), custom_call_target="tpu_custom_call" | custom-call | tf_op jit(solution)/shard_map/tree_attention/pallas_call | solution.py:615
  57.9 3.8 %hand_over.1 = (bf16[128,4096]{1,0:T(8,128)(2,1)}, bf16[128,4096]{1,0:T(8,128)(2,1)}, bf16[128,1024]{1,0:T(8,128)(2,1)}, bf16[32,256]{1,0:T(8,128)(2,1)}) custom-call(bf16[128,4096]{1,0:T(8,128)(2,1)} %get-tuple-element.12.a, bf16[128,4096]{1,0:T(8,128)(2,1)} %get-tuple-element.13.b, bf16[128,1024]{1,0:T(8,128)(2,1)} %get-tuple-element.14.c, ...), custom_call_target="tpu_custom_call" | custom-call | tf_op jit(solution)/shard_map/hand_over/pallas_call | solution.py:661

commit v6 on v5

--- a/solution.py
+++ b/solution.py
@@ -10,6 +10,7 @@
 
 HK = 4
 HD = 128
+PARTS = 2
 F32 = jnp.float32
 BF16 = jnp.bfloat16
 
@@ -36,41 +37,48 @@
     def heads(x):
         return [x[:, h * HD:(h + 1) * HD] for h in range(group)]
 
-    query_rows = jnp.concatenate(heads(query), axis=0)
-    grad_rows = jnp.concatenate(heads(grad_live), axis=0)
-    grad_cols = jnp.concatenate([h.T for h in heads(grad_live)], axis=1)
-
-    scores = lax.dot_general(keys, query_rows, (((1,), (1,)), ((), ())), preferred_element_type=F32)
     row = lax.broadcasted_iota(jnp.int32, (block, block), 1)
     key = lax.broadcasted_iota(jnp.int32, (block, block), 0)
+    part = group // PARTS
     own_bias = jnp.where((key < own_length) & (key <= row), 0.0, -jnp.inf)
-    own_bias = jnp.concatenate([own_bias] * group, axis=1)
-    parts = [scores[:prefix_rows], scores[prefix_rows:prefix_rows + block] + own_bias]
-    for s, length in enumerate(slot_lengths):
-        first = prefix_rows + (s + 1) * block
-        parts.append(scores[first:first + block] + jnp.where(place < length, 0.0, -jnp.inf))
-    scores = jnp.concatenate(parts, axis=0)
-    top = jnp.max(scores, axis=0, keepdims=True) * to_exp2
-    exponent = jnp.exp2(scores * to_exp2 - top)
-    probs = exponent * (1.0 / jnp.sum(exponent, axis=0, keepdims=True))
-    probs_low = probs.astype(BF16)
-    attended = lax.dot_general(values, probs_low, (((0,), (0,)), ((), ())), preferred_element_type=F32)
+    own_bias = jnp.concatenate([own_bias] * part, axis=1)
+    slot_bias = [jnp.where(place < length, 0.0, -jnp.inf) for length in slot_lengths]
     live = lax.broadcasted_iota(jnp.int32, (1, block), 1) < own_length
-    live = jnp.concatenate([jnp.where(live, 1.0, 0.0)] * group, axis=1)
-    attended = (attended * live).astype(BF16)
-    delta = jnp.sum(grad_cols.astype(F32) * attended.astype(F32), axis=0, keepdims=True)
-    grad_probs = jnp.dot(values, grad_cols, preferred_element_type=F32)
-    grad_scores = (probs * (grad_probs - delta)).astype(BF16)
-    grad_query = lax.dot_general(keys, grad_scores, (((0,), (0,)), ((), ())), preferred_element_type=F32)
-    grad_query = (grad_query * scale).astype(BF16)
-    grad_keys = jnp.dot(grad_scores, query_rows, preferred_element_type=F32) * scale
-    grad_values = jnp.dot(probs_low, grad_rows, preferred_element_type=F32)
-    return (
-        jnp.concatenate([h.T for h in heads_across(attended, block)], axis=1),
-        jnp.concatenate([h.T for h in heads_across(grad_query, block)], axis=1),
-        grad_keys,
-        grad_values,
-    )
+    live = jnp.concatenate([jnp.where(live, 1.0, 0.0)] * part, axis=1)
+
+    def softmax(scores):
+        parts = [scores[:prefix_rows], scores[prefix_rows:prefix_rows + block] + own_bias]
+        for s, bias in enumerate(slot_bias):
+            first = prefix_rows + (s + 1) * block
+            parts.append(scores[first:first + block] + bias)
+        scores = jnp.concatenate(parts, axis=0)
+        top = jnp.max(scores, axis=0, keepdims=True) * to_exp2
+        exponent = jnp.exp2(scores * to_exp2 - top)
+        return exponent * (1.0 / jnp.sum(exponent, axis=0, keepdims=True))
+
+    def dot(x, y, over):
+        return lax.dot_general(x, y, (over, ((), ())), preferred_element_type=F32)
+
+    all_queries, all_grads = heads(query), heads(grad_live)
+    taken = [slice(p * part, (p + 1) * part) for p in range(PARTS)]
+    query_rows = [jnp.concatenate(all_queries[t], axis=0) for t in taken]
+    grad_rows = [jnp.concatenate(all_grads[t], axis=0) for t in taken]
+    grad_cols = [jnp.concatenate([h.T for h in all_grads[t]], axis=1) for t in taken]
+    scores = [dot(keys, q, ((1,), (1,))) for q in query_rows]
+    out, d_query, grad_keys, grad_values = [], [], 0.0, 0.0
+    for p in range(PARTS):
+        grad_probs = dot(values, grad_cols[p], ((1,), (0,)))
+        probs = softmax(scores[p])
+        probs_low = probs.astype(BF16)
+        attended = (dot(values, probs_low, ((0,), (0,))) * live).astype(BF16)
+        delta = jnp.sum(grad_cols[p].astype(F32) * attended.astype(F32), axis=0, keepdims=True)
+        grad_scores = (probs * (grad_probs - delta)).astype(BF16)
+        grad_query = (dot(keys, grad_scores, ((0,), (0,))) * scale).astype(BF16)
+        grad_keys += dot(grad_scores, query_rows[p], ((1,), (0,)))
+        grad_values += dot(probs_low, grad_rows[p], ((1,), (0,)))
+        out += [h.T for h in heads_across(attended, block)]
+        d_query += [h.T for h in heads_across(grad_query, block)]
+    return jnp.concatenate(out, axis=1), jnp.concatenate(d_query, axis=1), grad_keys * scale, grad_values
 
 
 def heads_across(x, block):
@@ -656,11 +664,11 @@
         ),
         name="tree_attention",
     )(parents, lengths, query[0], d_out[0], branch_kv[0], prefix_kv)
-    rows = [pl.BlockSpec((x.shape[0] // HK, x.shape[1]), lambda r: (r, 0)) for x in results[:3]]
+    rows = [pl.BlockSpec((x.shape[0] // 2, x.shape[1]), lambda r: (r, 0)) for x in results[:3]]
     rows.append(pl.BlockSpec(results[3].shape, lambda r: (0, 0)))
     out, d_query, d_branch, d_prefix = pl.pallas_call(
         hand_over_kernel,
-        grid=(HK,),
+        grid=(2,),
         in_specs=rows,
         out_specs=rows,
         out_shape=[jax.ShapeDtypeStruct(x.shape, x.dtype) for x in results],

time: 61.9 us -> 62.3 us (level)
    pallas_call x1, Pallas kernels: 57.3 us -> 58.6 us  [per_device(): pl.pallas_call(functools.partial(tree_kernel, ctx_size, smp_size), in_spe...]
    pallas_call x1, Pallas kernels: 3.83 us -> 2.87 us  [per_device(): pl.pallas_call(hand_over_kernel, grid=(2,), in_specs=rows, out_specs=rows...]
where the time goes in v6:
time: 62.3 us; the launch traced here: 62.1 us
  Pallas kernels  61.5 us (99%)
  between operations  0.64 us (1%)
    pallas_call x1, Pallas kernels, per_device(): pl.pallas_call(functools.partial(tree_kernel, ctx_size, smp_size), in_spe...  58.6 us
    pallas_call x1, Pallas kernels, per_device(): pl.pallas_call(hand_over_kernel, grid=(2,), in_specs=rows, out_specs=rows...  2.87 us

profile of v6, /device:TPU:0, one launch (start us, length us, event | category | flops | bytes accessed | tf_op | source)
XLA Modules:
  0.0 62.1 jit_solution(17538969669888494786)
XLA Ops:
  0.6 58.6 %tree_attention.1 = (bf16[128,4096]{1,0:T(8,128)(2,1)}, bf16[128,4096]{1,0:T(8,128)(2,1)}, bf16[128,1024]{1,0:T(8,128)(2,1)}, bf16[32,256]{1,0:T(8,128)(2,1)}) custom-call(s32[1,8]{1,0:T(1,128)} %parents.1, s32[1,8]{1,0:T(1,128)} %lengths.1, bf16[128,4096]{1,0:T(8,128)(2,1)} %bitcast.6, bf16[128,4096]{1,0:T(8,128)(2,1)} %bitcast.7, ...), custom_call_target="tpu_custom_call" | custom-call | tf_op jit(solution)/shard_map/tree_attention/pallas_call | solution.py:623
  59.2 2.9 %hand_over.1 = (bf16[128,4096]{1,0:T(8,128)(2,1)}, bf16[128,4096]{1,0:T(8,128)(2,1)}, bf16[128,1024]{1,0:T(8,128)(2,1)}, bf16[32,256]{1,0:T(8,128)(2,1)}) custom-call(bf16[128,4096]{1,0:T(8,128)(2,1)} %get-tuple-element.12.a, bf16[128,4096]{1,0:T(8,128)(2,1)} %get-tuple-element.13.b, bf16[128,1024]{1,0:T(8,128)(2,1)} %get-tuple-element.14.c, ...), custom_call_target="tpu_custom_call" | custom-call | tf_op jit(solution)/shard_map/hand_over/pallas_call | solution.py:669

commit v7 on v5

--- a/solution.py
+++ b/solution.py
@@ -656,11 +656,11 @@
         ),
         name="tree_attention",
     )(parents, lengths, query[0], d_out[0], branch_kv[0], prefix_kv)
-    rows = [pl.BlockSpec((x.shape[0] // HK, x.shape[1]), lambda r: (r, 0)) for x in results[:3]]
+    rows = [pl.BlockSpec((x.shape[0] // 2, x.shape[1]), lambda r: (r, 0)) for x in results[:3]]
     rows.append(pl.BlockSpec(results[3].shape, lambda r: (0, 0)))
     out, d_query, d_branch, d_prefix = pl.pallas_call(
         hand_over_kernel,
-        grid=(HK,),
+        grid=(2,),
         in_specs=rows,
         out_specs=rows,
         out_shape=[jax.ShapeDtypeStruct(x.shape, x.dtype) for x in results],

time: 61.9 us -> 61 us (0.985)
  Pallas kernels: 61.1 us -> 60.1 us
    pallas_call x1, Pallas kernels: 3.83 us -> 2.87 us  [per_device(): pl.pallas_call(hand_over_kernel, grid=(2,), in_specs=rows, out_specs=rows...]
where the time goes in v7:
time: 61 us; the launch traced here: 60.8 us
  Pallas kernels  60.1 us (99%)
  between operations  0.64 us (1%)
    pallas_call x1, Pallas kernels, per_device(): pl.pallas_call(functools.partial(tree_kernel, ctx_size, smp_size), in_spe...  57.3 us
    pallas_call x1, Pallas kernels, per_device(): pl.pallas_call(hand_over_kernel, grid=(2,), in_specs=rows, out_specs=rows...  2.87 us

profile of v7, /device:TPU:0, one launch (start us, length us, event | category | flops | bytes accessed | tf_op | source)
XLA Modules:
  0.0 60.8 jit_solution(6197314942127998482)
XLA Ops:
  0.6 57.3 %tree_attention.1 = (bf16[128,4096]{1,0:T(8,128)(2,1)}, bf16[128,4096]{1,0:T(8,128)(2,1)}, bf16[128,1024]{1,0:T(8,128)(2,1)}, bf16[32,256]{1,0:T(8,128)(2,1)}) custom-call(s32[1,8]{1,0:T(1,128)} %parents.1, s32[1,8]{1,0:T(1,128)} %lengths.1, bf16[128,4096]{1,0:T(8,128)(2,1)} %bitcast.6, bf16[128,4096]{1,0:T(8,128)(2,1)} %bitcast.7, ...), custom_call_target="tpu_custom_call" | custom-call | tf_op jit(solution)/shard_map/tree_attention/pallas_call | solution.py:615
  57.9 2.9 %hand_over.1 = (bf16[128,4096]{1,0:T(8,128)(2,1)}, bf16[128,4096]{1,0:T(8,128)(2,1)}, bf16[128,1024]{1,0:T(8,128)(2,1)}, bf16[32,256]{1,0:T(8,128)(2,1)}) custom-call(bf16[128,4096]{1,0:T(8,128)(2,1)} %get-tuple-element.12.a, bf16[128,4096]{1,0:T(8,128)(2,1)} %get-tuple-element.13.b, bf16[128,1024]{1,0:T(8,128)(2,1)} %get-tuple-element.14.c, ...), custom_call_target="tpu_custom_call" | custom-call | tf_op jit(solution)/shard_map/hand_over/pallas_call | solution.py:661
